TPU v7x, 32 devices: a whole 2x2x4 slice. The times are simulated.
32 devices in a mesh: dp: 4 (over y, x), seq: 8 (over z, core).
Axes of the slice: x: 2, y: 2, z: 4, core: 2. Of those that a mesh axis runs over, the one named last changes fastest.
Arguments:
- hidden_in: bfloat16 [8, 4096, 1024], P('dp', 'seq'), may hold values from -6 to 6
- segment_ids: int32 [8, 4096], P('dp'), may hold values from 0 to 256, as said below
- query_weight: bfloat16 [1024, 1024], P(('dp', 'seq')), may hold values from -0.1875 to 0.1875
- query_bias: bfloat16 [1024], P(('dp', 'seq')), may hold values from -3 to 3
- key_weight: bfloat16 [1024, 1024], P(('dp', 'seq')), may hold values from -0.1875 to 0.1875
- value_weight: bfloat16 [1024, 1024], P(('dp', 'seq')), may hold values from -0.1875 to 0.1875
- value_bias: bfloat16 [1024], P(('dp', 'seq')), may hold values from -3 to 3
- output_weight: bfloat16 [1024, 1024], P(('dp', 'seq')), may hold values from -0.5 to 0.5
- output_bias: bfloat16 [1024], P(('dp', 'seq')), may hold values from -3 to 3
- first_gain: bfloat16 [1024], P(('dp', 'seq')), may hold values from 0.5 to 1.5
- first_shift: bfloat16 [1024], P(('dp', 'seq')), may hold values from -3 to 3
- inner_weight: bfloat16 [1024, 4096], P(('dp', 'seq')), may hold values from -0.1875 to 0.1875
- inner_bias: bfloat16 [4096], P(('dp', 'seq')), may hold values from -3 to 3
- outer_weight: bfloat16 [4096, 1024], P(('dp', 'seq')), may hold values from -0.09375 to 0.09375
- outer_bias: bfloat16 [1024], P(('dp', 'seq')), may hold values from -3 to 3
- second_gain: bfloat16 [1024], P(('dp', 'seq')), may hold values from 0.5 to 1.5
- second_shift: bfloat16 [1024], P(('dp', 'seq')), may hold values from -3 to 3
- cotangent: bfloat16 [8, 4096, 1024], P('dp', 'seq'), may hold values from -6 to 6
Outputs:
- layer_out: bfloat16 [8, 4096, 1024], P('dp', 'seq')
- grad_hidden: float32 [8, 4096, 1024], P('dp', 'seq')
- query_weight_grad: float32 [1024, 1024], P(('dp', 'seq'))
- query_bias_grad: float32 [1024], P(('dp', 'seq'))
- key_weight_grad: float32 [1024, 1024], P(('dp', 'seq'))
- value_weight_grad: float32 [1024, 1024], P(('dp', 'seq'))
- value_bias_grad: float32 [1024], P(('dp', 'seq'))
- output_weight_grad: float32 [1024, 1024], P(('dp', 'seq'))
- output_bias_grad: float32 [1024], P(('dp', 'seq'))
- first_gain_grad: float32 [1024], P(('dp', 'seq'))
- first_shift_grad: float32 [1024], P(('dp', 'seq'))
- inner_weight_grad: float32 [1024, 4096], P(('dp', 'seq'))
- inner_bias_grad: float32 [4096], P(('dp', 'seq'))
- outer_weight_grad: float32 [4096, 1024], P(('dp', 'seq'))
- outer_bias_grad: float32 [1024], P(('dp', 'seq'))
- second_gain_grad: float32 [1024], P(('dp', 'seq'))
- second_shift_grad: float32 [1024], P(('dp', 'seq'))
Inputs may be any that keep to these rules, and one draw needn't show every extreme that they name: `segment_ids`: ids never fall along a row and restart for each row; the tokens of a segment are contiguous and its id is positive; 0 marks padding at a row's end, and every row ends in padding. Each segment holds 16 to 256 tokens, a row's first exactly 256, and no segment other than a row's first starts at a position divisible by 512. A row's last segment has the id 4096 // 16.
All inputs are finite; a program needn't handle non-finite values.
Results may differ from a plain program's by a relative error of at most 0.014.
Values may be sent and summed in bfloat16 or wider, within the bound.
A program may use at most 256 MiB of HBM per device.

v0:
```python
import jax
import jax.numpy as jnp
from jax import lax
from jax.sharding import PartitionSpec as P

HD = 64
SEGMAX = 256


group_heads = 4


def passed_along(block, axis, distance):
    devices = range(lax.axis_size(axis))
    route = [(i - distance, i) for i in devices if i - distance in devices]
    return lax.ppermute(block, axis, route)


def normalize(hidden, gain, shift):
    center = hidden - jnp.mean(hidden, axis=-1, keepdims=True)
    spread = jnp.mean(center * center, axis=-1, keepdims=True)
    return center * lax.rsqrt(spread + 1e-05) * gain + shift


def contract_rows(left, right):
    return lax.dot_general(
        left, right, (((0,), (0,)), ((), ())), preferred_element_type=jnp.float32
    )


def times_transposed(left, right):
    return lax.dot_general(
        left, right, (((1,), (1,)), ((), ())), preferred_element_type=jnp.float32
    )


def column_sum(values):
    return jnp.sum(values.astype(jnp.float32), axis=0)


def local(
    hidden_in,
    segment_ids,
    query_weight,
    query_bias,
    key_weight,
    value_weight,
    value_bias,
    output_weight,
    output_bias,
    first_gain,
    first_shift,
    inner_weight,
    inner_bias,
    outer_weight,
    outer_bias,
    second_gain,
    second_shift,
    cotangent,
):
    rows_here, tokens, width = hidden_in.shape
    window = tokens + SEGMAX
    span = group_heads * HD
    groups = width // span
    items = jnp.arange(rows_here * groups, dtype=jnp.int32)
    (
        query_matrix,
        query_offset,
        key_matrix,
        value_matrix,
        value_offset,
        output_matrix,
        output_offset,
        first_scale,
        first_offset,
    ) = (
        lax.all_gather(query_weight, ("dp", "seq"), axis=0, tiled=True),
        lax.all_gather(query_bias, ("dp", "seq"), axis=0, tiled=True),
        lax.all_gather(key_weight, ("dp", "seq"), axis=0, tiled=True),
        lax.all_gather(value_weight, ("dp", "seq"), axis=0, tiled=True),
        lax.all_gather(value_bias, ("dp", "seq"), axis=0, tiled=True),
        lax.all_gather(output_weight, ("dp", "seq"), axis=0, tiled=True),
        lax.all_gather(output_bias, ("dp", "seq"), axis=0, tiled=True),
        lax.all_gather(first_gain, ("dp", "seq"), axis=0, tiled=True),
        lax.all_gather(first_shift, ("dp", "seq"), axis=0, tiled=True),
    )
    flat = hidden_in.reshape(rows_here * tokens, width)
    offset = lax.axis_index("seq") * tokens
    padded_ids = jnp.concatenate(
        [jnp.full((rows_here, SEGMAX), -1, jnp.int32), segment_ids], axis=1
    )
    key_ids = lax.dynamic_slice_in_dim(padded_ids, offset, window, 1)
    query_ids = key_ids[:, SEGMAX:]
    diagonal = jnp.arange(window)[None, :] == jnp.arange(tokens)[:, None] + SEGMAX
    visible = (query_ids[:, :, None] == key_ids[:, None, :]) & (
        query_ids[:, :, None] > 0
    ) | diagonal[None]
    queries = (
        (
            jnp.dot(flat, query_matrix, preferred_element_type=jnp.float32)
            + query_offset.astype(jnp.float32)
        )
        .astype(jnp.bfloat16)
        .reshape(rows_here, tokens, width)
    )
    keys_own = (
        jnp.dot(flat, key_matrix, preferred_element_type=jnp.float32)
        .astype(jnp.bfloat16)
        .reshape(rows_here, tokens, width)
    )
    values_own = (
        (
            jnp.dot(flat, value_matrix, preferred_element_type=jnp.float32)
            + value_offset.astype(jnp.float32)
        )
        .astype(jnp.bfloat16)
        .reshape(rows_here, tokens, width)
    )
    tails = passed_along(
        (keys_own[:, tokens - SEGMAX :], values_own[:, tokens - SEGMAX :]), "seq", 1
    )
    keys_all = jnp.concatenate([tails[0], keys_own], axis=1)
    values_all = jnp.concatenate([tails[1], values_own], axis=1)

    def pieces(item):
        row = item // groups
        column = item % groups * span
        query_part = lax.dynamic_slice(queries, (row, 0, column), (1, tokens, span))[0].reshape(
            tokens, group_heads, HD
        )
        key_part = lax.dynamic_slice(keys_all, (row, 0, column), (1, window, span))[0].reshape(
            window, group_heads, HD
        )
        value_part = lax.dynamic_slice(values_all, (row, 0, column), (1, window, span))[0].reshape(
            window, group_heads, HD
        )
        mask_row = lax.dynamic_index_in_dim(visible, row, 0, keepdims=False)
        scores = (
            jnp.einsum("qhd,khd->hqk", query_part, key_part, preferred_element_type=jnp.float32)
            * 0.125
        )
        scores = jnp.where(mask_row[None], scores, -1e30)
        return (row, column, query_part, key_part, value_part, scores)

    def attend(item):
        row, column, query_part, key_part, value_part, scores = pieces(item)
        highest = jnp.max(scores, axis=-1, keepdims=True)
        expo = jnp.exp(scores - highest)
        total = jnp.sum(expo, axis=-1, keepdims=True)
        probs = (expo / total).astype(jnp.bfloat16)
        mixed_part = jnp.einsum(
            "hqk,khd->qhd", probs, value_part, preferred_element_type=jnp.float32
        )
        return (
            mixed_part.astype(jnp.bfloat16).reshape(tokens, span),
            highest[..., 0] + jnp.log(total[..., 0]),
        )

    mixed_parts, logsums = lax.map(attend, items)
    mixed = (
        mixed_parts.reshape(rows_here, groups, tokens, span)
        .transpose(0, 2, 1, 3)
        .reshape(rows_here * tokens, width)
    )
    first_sum = (
        flat.astype(jnp.float32)
        + jnp.dot(mixed, output_matrix, preferred_element_type=jnp.float32)
        + output_offset.astype(jnp.float32)
    )
    normed = normalize(first_sum, first_scale.astype(jnp.float32), first_offset.astype(jnp.float32))
    normed_low = normed.astype(jnp.bfloat16)
    inner_matrix, inner_offset, outer_matrix, outer_offset, second_scale, second_offset = (
        lax.all_gather(inner_weight, ("dp", "seq"), axis=0, tiled=True),
        lax.all_gather(inner_bias, ("dp", "seq"), axis=0, tiled=True),
        lax.all_gather(outer_weight, ("dp", "seq"), axis=0, tiled=True),
        lax.all_gather(outer_bias, ("dp", "seq"), axis=0, tiled=True),
        lax.all_gather(second_gain, ("dp", "seq"), axis=0, tiled=True),
        lax.all_gather(second_shift, ("dp", "seq"), axis=0, tiled=True),
    )
    inner = jnp.dot(
        normed_low, inner_matrix, preferred_element_type=jnp.float32
    ) + inner_offset.astype(jnp.float32)
    active_low = jax.nn.gelu(inner, approximate=False).astype(jnp.bfloat16)
    second_sum = (
        normed
        + jnp.dot(active_low, outer_matrix, preferred_element_type=jnp.float32)
        + outer_offset.astype(jnp.float32)
    )
    layer_out = normalize(
        second_sum, second_scale.astype(jnp.float32), second_offset.astype(jnp.float32)
    )
    layer_out = layer_out.astype(jnp.bfloat16).reshape(rows_here, tokens, width)
    inner_matrix, inner_offset, outer_matrix, outer_offset, second_scale, second_offset = (
        lax.all_gather(inner_weight, ("dp", "seq"), axis=0, tiled=True),
        lax.all_gather(inner_bias, ("dp", "seq"), axis=0, tiled=True),
        lax.all_gather(outer_weight, ("dp", "seq"), axis=0, tiled=True),
        lax.all_gather(outer_bias, ("dp", "seq"), axis=0, tiled=True),
        lax.all_gather(second_gain, ("dp", "seq"), axis=0, tiled=True),
        lax.all_gather(second_shift, ("dp", "seq"), axis=0, tiled=True),
    )
    upstream = cotangent.reshape(rows_here * tokens, width).astype(jnp.float32)
    _, pull_second = jax.vjp(
        normalize, second_sum, second_scale.astype(jnp.float32), second_offset.astype(jnp.float32)
    )
    grad_second, second_gain_grad, second_shift_grad = pull_second(upstream)
    outer_grad = grad_second.astype(jnp.bfloat16)
    outer_weight_grad = contract_rows(active_low, outer_grad)
    outer_bias_grad = column_sum(outer_grad)
    _, pull_gelu = jax.vjp(lambda value: jax.nn.gelu(value, approximate=False), inner)
    (inner_grad_full,) = pull_gelu(times_transposed(outer_grad, outer_matrix))
    inner_grad = inner_grad_full.astype(jnp.bfloat16)
    inner_weight_grad = contract_rows(normed_low, inner_grad)
    inner_bias_grad = column_sum(inner_grad)
    grad_normed = grad_second + times_transposed(inner_grad, inner_matrix)
    (
        query_matrix,
        query_offset,
        key_matrix,
        value_matrix,
        value_offset,
        output_matrix,
        output_offset,
        first_scale,
        first_offset,
    ) = (
        lax.all_gather(query_weight, ("dp", "seq"), axis=0, tiled=True),
        lax.all_gather(query_bias, ("dp", "seq"), axis=0, tiled=True),
        lax.all_gather(key_weight, ("dp", "seq"), axis=0, tiled=True),
        lax.all_gather(value_weight, ("dp", "seq"), axis=0, tiled=True),
        lax.all_gather(value_bias, ("dp", "seq"), axis=0, tiled=True),
        lax.all_gather(output_weight, ("dp", "seq"), axis=0, tiled=True),
        lax.all_gather(output_bias, ("dp", "seq"), axis=0, tiled=True),
        lax.all_gather(first_gain, ("dp", "seq"), axis=0, tiled=True),
        lax.all_gather(first_shift, ("dp", "seq"), axis=0, tiled=True),
    )
    _, pull_first = jax.vjp(
        normalize, first_sum, first_scale.astype(jnp.float32), first_offset.astype(jnp.float32)
    )
    grad_first, first_gain_grad, first_shift_grad = pull_first(grad_normed)
    attn_grad = grad_first.astype(jnp.bfloat16)
    output_weight_grad = contract_rows(mixed, attn_grad)
    output_bias_grad = column_sum(attn_grad)
    grad_mixed = (
        times_transposed(attn_grad, output_matrix)
        .astype(jnp.bfloat16)
        .reshape(rows_here, tokens, width)
    )

    def attend_back(item):
        row, column, query_part, key_part, value_part, scores = pieces(item)
        logsum = lax.dynamic_index_in_dim(logsums, item, 0, keepdims=False)
        grad_part = lax.dynamic_slice(grad_mixed, (row, 0, column), (1, tokens, span))[0].reshape(
            tokens, group_heads, HD
        )
        probs = jnp.exp(scores - logsum[..., None])
        dprob = jnp.einsum(
            "qhd,khd->hqk", grad_part, value_part, preferred_element_type=jnp.float32
        )
        delta = jnp.sum(probs * dprob, axis=-1, keepdims=True)
        score_grad = (probs * (dprob - delta)).astype(jnp.bfloat16)
        query_part_grad = (
            jnp.einsum("hqk,khd->qhd", score_grad, key_part, preferred_element_type=jnp.float32)
            * 0.125
        )
        key_part_grad = (
            jnp.einsum("hqk,qhd->khd", score_grad, query_part, preferred_element_type=jnp.float32)
            * 0.125
        )
        value_part_grad = jnp.einsum(
            "hqk,qhd->khd",
            probs.astype(jnp.bfloat16),
            grad_part,
            preferred_element_type=jnp.float32,
        )
        return (
            query_part_grad.reshape(tokens, span),
            key_part_grad.reshape(window, span),
            value_part_grad.reshape(window, span),
        )

    query_parts, key_parts, value_parts = lax.map(attend_back, items)
    query_full = (
        query_parts.reshape(rows_here, groups, tokens, span)
        .transpose(0, 2, 1, 3)
        .reshape(rows_here * tokens, width)
    )
    key_window = (
        key_parts.reshape(rows_here, groups, window, span)
        .transpose(0, 2, 1, 3)
        .reshape(rows_here, window, width)
    )
    value_window = (
        value_parts.reshape(rows_here, groups, window, span)
        .transpose(0, 2, 1, 3)
        .reshape(rows_here, window, width)
    )
    returned = (
        passed_along(key_window[:, :SEGMAX].astype(jnp.bfloat16), "seq", -1).astype(jnp.float32),
        passed_along(value_window[:, :SEGMAX].astype(jnp.bfloat16), "seq", -1).astype(jnp.float32),
    )
    key_own = key_window[:, SEGMAX:]
    value_own = value_window[:, SEGMAX:]
    key_total = jnp.concatenate(
        [key_own[:, : tokens - SEGMAX], key_own[:, tokens - SEGMAX :] + returned[0]], axis=1
    )
    value_total = jnp.concatenate(
        [value_own[:, : tokens - SEGMAX], value_own[:, tokens - SEGMAX :] + returned[1]], axis=1
    )
    query_grad = query_full.astype(jnp.bfloat16)
    key_grad = key_total.reshape(rows_here * tokens, width).astype(jnp.bfloat16)
    value_grad = value_total.reshape(rows_here * tokens, width).astype(jnp.bfloat16)
    query_weight_grad = contract_rows(flat, query_grad)
    query_bias_grad = column_sum(query_grad)
    key_weight_grad = contract_rows(flat, key_grad)
    value_weight_grad = contract_rows(flat, value_grad)
    value_bias_grad = column_sum(value_grad)
    grad_hidden = (
        grad_first
        + times_transposed(query_grad, query_matrix)
        + times_transposed(key_grad, key_matrix)
        + times_transposed(value_grad, value_matrix)
    ).reshape(rows_here, tokens, width)
    shards = (
        lax.psum_scatter(query_weight_grad, ("dp", "seq"), scatter_dimension=0, tiled=True),
        lax.psum_scatter(query_bias_grad, ("dp", "seq"), scatter_dimension=0, tiled=True),
        lax.psum_scatter(key_weight_grad, ("dp", "seq"), scatter_dimension=0, tiled=True),
        lax.psum_scatter(value_weight_grad, ("dp", "seq"), scatter_dimension=0, tiled=True),
        lax.psum_scatter(value_bias_grad, ("dp", "seq"), scatter_dimension=0, tiled=True),
        lax.psum_scatter(output_weight_grad, ("dp", "seq"), scatter_dimension=0, tiled=True),
        lax.psum_scatter(output_bias_grad, ("dp", "seq"), scatter_dimension=0, tiled=True),
        lax.psum_scatter(first_gain_grad, ("dp", "seq"), scatter_dimension=0, tiled=True),
        lax.psum_scatter(first_shift_grad, ("dp", "seq"), scatter_dimension=0, tiled=True),
        lax.psum_scatter(inner_weight_grad, ("dp", "seq"), scatter_dimension=0, tiled=True),
        lax.psum_scatter(inner_bias_grad, ("dp", "seq"), scatter_dimension=0, tiled=True),
        lax.psum_scatter(outer_weight_grad, ("dp", "seq"), scatter_dimension=0, tiled=True),
        lax.psum_scatter(outer_bias_grad, ("dp", "seq"), scatter_dimension=0, tiled=True),
        lax.psum_scatter(second_gain_grad, ("dp", "seq"), scatter_dimension=0, tiled=True),
        lax.psum_scatter(second_shift_grad, ("dp", "seq"), scatter_dimension=0, tiled=True),
    )
    return (
        layer_out,
        grad_hidden,
        shards[0],
        shards[1],
        shards[2],
        shards[3],
        shards[4],
        shards[5],
        shards[6],
        shards[7],
        shards[8],
        shards[9],
        shards[10],
        shards[11],
        shards[12],
        shards[13],
        shards[14],
    )


def solution(mesh):
    in_specs = (
        P("dp", "seq", None),
        P("dp", None),
        P(("dp", "seq"), None),
        P(("dp", "seq")),
        P(("dp", "seq"), None),
        P(("dp", "seq"), None),
        P(("dp", "seq")),
        P(("dp", "seq"), None),
        P(("dp", "seq")),
        P(("dp", "seq")),
        P(("dp", "seq")),
        P(("dp", "seq"), None),
        P(("dp", "seq")),
        P(("dp", "seq"), None),
        P(("dp", "seq")),
        P(("dp", "seq")),
        P(("dp", "seq")),
        P("dp", "seq", None),
    )
    out_specs = (
        P("dp", "seq", None),
        P("dp", "seq", None),
        P(("dp", "seq"), None),
        P(("dp", "seq")),
        P(("dp", "seq"), None),
        P(("dp", "seq"), None),
        P(("dp", "seq")),
        P(("dp", "seq"), None),
        P(("dp", "seq")),
        P(("dp", "seq")),
        P(("dp", "seq")),
        P(("dp", "seq"), None),
        P(("dp", "seq")),
        P(("dp", "seq"), None),
        P(("dp", "seq")),
        P(("dp", "seq")),
        P(("dp", "seq")),
    )
    return jax.shard_map(local, mesh=mesh, in_specs=in_specs, out_specs=out_specs, check_vma=False)
```

profile of v0, /device:TPU:0, one launch (start us, length us, event | category | flops | bytes accessed | tf_op | source)
XLA Modules:
  0.0 1514.9 jit_solution(9357302610576171015)
XLA Ops:
  18.0 42.3 %all-reduce.19 = (bf16[1024]{0:T(1024)(128)(2,1)S(1)}, bf16[1024]{0:T(1024)(128)(2,1)S(1)}, bf16[1024]{0:T(1024)(128)(2,1)S(1)}, bf16[1024]{0:T(1024)(128)(2,1)S...) all-reduce(bf16[1024]{0:T(1024)(128)(2,1)S(1)} %dynamic-update-slic, ...), channel_id=1, replica_groups=mesh['dp'=4,'seq'=8] {'dp','seq'}, use_global_device_ids=true, to_apply=%add.3 | all-reduce | flops 8192 | bytes 32768
  62.0 40.4 %all-gather = bf16[32,1,128]{2,1,0:T(2,128)(2,1)S(1)} all-gather(bf16[1,1,128]{2,1,0:T(2,128)(2,1)} %bitcast.232), channel_id=1, replica_groups=mesh['dp'=4,'seq'=8] {'dp','seq'}, dimensions={0}, use_global_device_ids=true | all-gather | bytes 8448 | tf_op jit(solution)/shard_map/all_gather | solution.py:174
  104.2 5.9 add_convert_fusion.3
  110.1 2.9 copy.59
  114.0 3.2 collective-permute-start
  117.2 11.7 all-gather.12.cloned.1.call-done
  128.9 5.9 convolution_convert_fusion.1
  134.7 3.9 copy.61
  141.0 3.4 collective-permute-start.1
  145.2 42.4 %all-gather.10.cloned.1.call-done = bf16[1024,1024]{1,0:T(8,128)(2,1)} async-done(((bf16[32,1024]{1,0:T(8,128)(2,1)}), bf16[1024,1024]{1,0:T(8,128)(2,1)}) %all-gather.10.cloned.1.call-update) | async-done | bytes 2097168 | tf_op jit(solution)/shard_map/all_gather | solution.py:77
  187.7 5.9 add_convert_fusion.2
  193.6 3.9 copy.63
  197.5 3.3 pad_maximum_fusion
  200.8 3.3 pad_maximum_fusion.1
  204.1 90.7 %while.30 = (s32[]{:T(128)}, bf16[8,512,256]{1,2,0:T(8,128)(2,1)S(1)}, f32[8,4,512]{2,1,0:T(4,128)}, s32[8]{0:T(128)S(1)}, bf16[2,768,1024]{1,2,0:T(8,128)(2,1)}...) while((s32[]{:T(128)}, ...), condition=%wide.region_3.4_spmd, body=%wide.region_0.3_spmd.sunk | while | flops 421656608 | bytes 24839108 | solution.py:159
  296.2 3.3 copy.64
  301.3 5.4 fusion.34
  309.9 15.2 %all-gather.16.cloned.1.call-done = bf16[1024,4096]{1,0:T(8,128)(2,1)} async-done(((bf16[32,4096]{1,0:T(8,128)(2,1)}), bf16[1024,4096]{1,0:T(8,128)(2,1)}) %all-gather.16.cloned.1.call-update) | async-done | bytes 8388624 | tf_op jit(solution)/shard_map/all_gather | solution.py:173
  325.1 51.6 %multiply_convert_fusion.1 = (bf16[1024,4096]{1,0:T(8,128)(2,1)}, f32[1024,4096]{1,0:T(8,128)}, f32[1024,4096]{1,0:T(8,128)}) fusion(f32[4096]{0:T(1024)S(1)} %bitcast.230, bf16[1024,4096]{1,0:T(8,128)(2,1)} %all-gather.16.cloned.1.call-done, f32[1024,1024]{1,0:T(8,128)} %copy-done.5, f32[1024]{0:T(1024)S(1)} %convert_element_type.162, ...), kind=kOutput, calls=%fused_computation.38 | convolution fusion | flops 8872001536 | bytes 54558720 | tf_op jit(solution)/shard_map/dot_general | solution.py:180
  376.7 27.3 %all-gather.18.cloned.1.call-done = bf16[4096,1024]{1,0:T(8,128)(2,1)} async-done(((bf16[128,1024]{1,0:T(8,128)(2,1)}), bf16[4096,1024]{1,0:T(8,128)(2,1)}) %all-gather.18.cloned.1.call-update) | async-done | bytes 8388624 | tf_op jit(solution)/shard_map/all_gather | solution.py:175
  404.0 14.8 fusion.35
  420.4 2.8 fusion.21
  423.2 3.2 fusion.30
  429.4 24.8 %convert_reduce_fusion = (f32[4096]{0:T(1024)}, bf16[1024,4096]{1,0:T(8,128)(2,1)}) fusion(f32[1024,4096]{1,0:T(8,128)} %get-tuple-element.450, f32[1024,4096]{1,0:T(8,128)} %get-tuple-element.468, f32[4096]{0:T(1024)S(1)} %bitcast.231, bf16[1024,1024]{1,0:T(8,128)(2,1)S(1)} %get-tuple-element.438, bf16[4096,1024]{1,0:T(8,128)(2,1)} %all-gather.18.cloned.1.call-done), kind=kOutput, calls=%fused_computation.36 | convolution fusion | flops 8661233664 | bytes 52461568 | tf_op jit(solution)/shard_map/dot_general | solution.py:32
  454.1 17.5 %multiply_reduce_fusion.1 = (f32[1024]{0:T(1024)}, f32[1024]{0:T(1024)S(1)}, f32[1024]{0:T(1024)}, f32[1024,1024]{1,0:T(8,128)S(1)}) fusion(f32[1024,1024]{1,0:T(8,128)} %copy-done.5, f32[1024]{0:T(1024)S(1)} %fusion.23, f32[1024]{0:T(1024)S(1)} %broadcast_multiply_fusion.1, f32[1024]{0:T(1024)S(1)} %convert_element_type.161, ...), kind=kOutput, calls=%fused_computation.64 | convolution fusion | flops 8600417280 | bytes 29388800 | tf_op jit(solution)/shard_map/dot_general | solution.py:32
  476.5 4.5 fusion.39
  481.1 5.3 convolution_convert_fusion
  486.4 206.1 %while.31 = (s32[]{:T(128)}, bf16[8,512,256]{1,2,0:T(8,128)(2,1)}, f32[8,768,256]{1,2,0:T(8,128)}, f32[8,768,256]{1,2,0:T(8,128)}, s32[8]{0:T(128)S(1)}, /*index...) while((s32[]{:T(128)}, bf16[8,512,256]{1,2,0:T(8,128)(2,1)}, ...), condition=%wide.region_14.15_spmd, body=%wide.region_12.14_spmd.sunk | while | flops 1030682624 | bytes 78964280 | solution.py:281
  492.0 3.7 fusion.120
  500.0 5.0 multiply_reduce_fusion.6
  517.7 3.7 fusion.120
  525.7 5.0 multiply_reduce_fusion.6
  543.5 3.7 fusion.120
  551.5 5.0 multiply_reduce_fusion.6
  569.3 3.7 fusion.120
  577.3 5.0 multiply_reduce_fusion.6
  595.0 3.7 fusion.120
  603.0 5.0 multiply_reduce_fusion.6
  620.7 3.7 fusion.120
  628.7 5.0 multiply_reduce_fusion.6
  646.4 3.7 fusion.120
  654.4 5.0 multiply_reduce_fusion.6
  672.0 3.7 fusion.120
  680.0 5.0 multiply_reduce_fusion.6
  692.5 3.0 copy.67
  697.4 4.4 convolution_bitcast_fusion.2
  701.7 5.4 copy.73
  707.2 2.6 fusion.33
  711.1 3.3 collective-permute-done.2
  717.4 4.4 convolution_bitcast_fusion.1
  721.8 5.4 copy.75
  731.3 20.5 %collective-permute-done.3 = bf16[2,256,1024]{1,2,0:T(8,128)(2,1)S(1)} collective-permute-done((bf16[2,256,1024]{1,2,0:T(8,128)(2,1)S(1)}, bf16[2,256,1024]{1,2,0:T(8,128)(2,1)S(1)}, u32[]{:S(2)}, u32[]{:S(2)}) %collective-permute-start.3) | collective-permute-done | bytes 1048608 | tf_op jit(solution)/shard_map/ppermute | solution.py:16
  755.5 4.3 convolution_bitcast_fusion
  759.7 5.4 copy.77
  765.8 16.8 %fusion.25 = f32[1024,4096]{1,0:T(8,128)} fusion(bf16[1024,4096]{1,0:T(8,128)(2,1)} %get-tuple-element.440, f32[1024,1024]{1,0:T(8,128)} %copy-done.5, f32[1024]{0:T(1024)S(1)} %copy-done.32, f32[1024]{0:T(1024)S(1)} %convert_element_type.161, f32[1024]{0:T(1024)S(1)} %fusion.23, f32[1024]{0:T(1024)S(1)} %broadcast_multiply_fusion.1), kind=kOutput, calls=%fused_computation.109 | convolution fusion | flops 8595177472 | bytes 29376512 | tf_op jit(solution)/shard_map/dot_general | solution.py:26
  782.8 16.2 %fusion.40 = f32[4096,1024]{1,0:T(8,128)} fusion(bf16[1024,4096]{1,0:T(8,128)(2,1)} %get-tuple-element.449, bf16[1024,1024]{1,0:T(8,128)(2,1)} %copy-done.12), kind=kOutput, calls=%fused_computation.121 | convolution fusion | flops 8589934592 | bytes 27262976 | tf_op jit(solution)/shard_map/dot_general | solution.py:26
  802.3 4.4 fusion.37
  809.3 60.3 %all-reduce.18 = (f32[1024]{0:T(1024)S(1)}, f32[1024]{0:T(1024)S(1)}, f32[1024]{0:T(1024)S(1)}, f32[1024]{0:T(1024)S(1)}, f32[1024]{0:T(1024)S(1)}, /*index=5*/f...) all-reduce(f32[1024]{0:T(1024)S(1)} %bitcast.229, ...), channel_id=3, replica_groups=mesh['dp'=4,'seq'=8] {'dp','seq'}, use_global_device_ids=true, to_apply=%region_17.18.clone | all-reduce | flops 12288 | bytes 98304
  878.7 4.8 fusion.38
  884.7 4.9 add_add_fusion.2
  889.5 102.6 %reduce-scatter.21.cloned.1.call-done = f32[32,1024]{1,0:T(8,128)} async-done(((f32[1024,1024]{1,0:T(8,128)}), f32[32,1024]{1,0:T(8,128)}) %reduce-scatter.21.cloned.1.call-update) | async-done | bytes 131088
  992.1 142.1 %reduce-scatter.23.cloned.1.call-done = f32[32,1024]{1,0:T(8,128)} async-done(((f32[1024,1024]{1,0:T(8,128)}), f32[32,1024]{1,0:T(8,128)}) %reduce-scatter.23.cloned.1.call-update) | async-done | bytes 131088
  1134.2 186.4 %reduce-scatter.15.cloned.1.call-done = f32[32,4096]{1,0:T(8,128)} async-done(((f32[1024,4096]{1,0:T(8,128)}), f32[32,4096]{1,0:T(8,128)}) %reduce-scatter.15.cloned.1.call-update) | async-done | bytes 524304 | tf_op jit(solution)/shard_map/reduce_scatter | solution.py:333
  1320.7 187.1 %reduce-scatter.17.cloned.1.call-done = f32[128,1024]{1,0:T(8,128)} async-done(((f32[4096,1024]{1,0:T(8,128)}), f32[128,1024]{1,0:T(8,128)}) %reduce-scatter.17.cloned.1.call-update) | async-done | bytes 524304 | tf_op jit(solution)/shard_map/reduce_scatter | solution.py:335
  (409 shorter events, 238.5 us)
Async XLA Ops:
  7.2 97.0 %all-gather.8.cloned.1.call-start = ((), (), s32[]{:S(2)}) async-start(), calls=%async_computation.6 | async-start | bytes 2162688 | tf_op jit(solution)/shard_map/all_gather | solution.py:80
  7.9 120.9 %all-gather.12.cloned.1.call-start = ((), (), s32[]{:S(2)}) async-start(), calls=%async_computation.8 | async-start | bytes 2162688 | tf_op jit(solution)/shard_map/all_gather | solution.py:79
  8.7 179.0 %all-gather.10.cloned.1.call-start = ((), (), s32[]{:S(2)}) async-start(), calls=%async_computation.7 | async-start | bytes 2162688 | tf_op jit(solution)/shard_map/all_gather | solution.py:77
  9.4 291.9 %all-gather.14.cloned.1.call-start = ((), (), s32[]{:S(2)}) async-start(), calls=%async_computation.9 | async-start | bytes 2162688 | tf_op jit(solution)/shard_map/all_gather | solution.py:82
  10.0 315.1 %all-gather.16.cloned.1.call-start = ((), (), s32[]{:S(2)}) async-start(), calls=%async_computation.10 | async-start | bytes 8650752 | tf_op jit(solution)/shard_map/all_gather | solution.py:173
  10.6 393.4 %all-gather.18.cloned.1.call-start = ((), (), s32[]{:S(2)}) async-start(), calls=%async_computation.11 | async-start | bytes 8650752 | tf_op jit(solution)/shard_map/all_gather | solution.py:175
  11.1 878.4 %reduce-scatter.13.cloned.1.call-start = ((), (), s32[]{:S(2)}) async-start(), calls=%async_computation.12 | async-start | bytes 4325376 | tf_op jit(solution)/shard_map/reduce_scatter | solution.py:329
  62.0 342.0 %copy-start.31 = (f32[1024]{0:T(1024)}, f32[1024]{0:T(1024)S(1)}, u32[]{:S(2)}) copy-start(f32[1024]{0:T(1024)S(1)} %convert_element_type.162) | copy-start | bytes 12292
  114.0 83.5 %collective-permute-start = (bf16[2,256,1024]{1,2,0:T(8,128)(2,1)}, bf16[2,256,1024]{1,2,0:T(8,128)(2,1)}, u32[]{:S(2)}, u32[]{:S(2)}) collective-permute-start(bf16[2,256,1024]{1,2,0:T(8,128)(2,1)} %slice.44), channel_id=1, source_target_pairs={{0,1},{1,2},{2,3},{3,4},{4,5},{5,6},{6,7},{8,9},{9,10},{10,11},{11... | collective-permute-start | bytes 3145736 | tf_op jit(solution)/shard_map/ppermute | solution.py:16
  141.0 59.8 %collective-permute-start.1 = (bf16[2,256,1024]{1,2,0:T(8,128)(2,1)}, bf16[2,256,1024]{1,2,0:T(8,128)(2,1)}, u32[]{:S(2)}, u32[]{:S(2)}) collective-permute-start(bf16[2,256,1024]{1,2,0:T(8,128)(2,1)} %slice.45), channel_id=1, source_target_pairs={{0,1},{1,2},{2,3},{3,4},{4,5},{5,6},{6,7},{8,9},{9,10},{10,11},{11... | collective-permute-start | bytes 3145736 | tf_op jit(solution)/shard_map/ppermute | solution.py:16
  197.5 3.3 copy-start.8
  200.8 3.3 copy-start.13
  294.8 6.5 copy-start
  306.7 2.0 copy-start.5
  325.1 78.9 %copy-start.33 = (f32[1024]{0:T(1024)S(1)}, f32[1024]{0:T(1024)}, u32[]{:S(2)}) copy-start(f32[1024]{0:T(1024)} %convert_element_type.166) | copy-start | bytes 12292
  419.4 3.8 copy-start.26
  426.4 2.0 copy-start.7
  429.4 24.8 %copy-start.12 = (bf16[1024,1024]{1,0:T(8,128)(2,1)}, bf16[1024,1024]{1,0:T(8,128)(2,1)S(1)}, u32[]{:S(2)}) copy-start(bf16[1024,1024]{1,0:T(8,128)(2,1)S(1)} %get-tuple-element.438) | copy-start | bytes 6291460
  454.1 17.5 %copy-start.21 = (f32[1024]{0:T(1024)S(1)}, f32[1024]{0:T(1024)}, u32[]{:S(2)}) copy-start(f32[1024]{0:T(1024)} %copy-done.20) | copy-start | bytes 12292
  454.1 17.5 %copy-start.6 = (f32[1024,1024]{1,0:T(8,128)S(1)}, f32[1024,1024]{1,0:T(8,128)}, u32[]{:S(2)}) copy-start(f32[1024,1024]{1,0:T(8,128)} %copy-done.5) | copy-start | bytes 12582916
  473.3 2.1 copy-start.3
  473.3 3.1 copy-start.17
  473.4 7.6 copy-start.24
  481.0 5.4 copy-start.1
  481.0 408.5 %reduce-scatter.19.cloned.1.call-start = ((), (), s32[]{:S(2)}) async-start(), calls=%async_computation.15 | async-start | bytes 4325376
  499.2 5.9 slice-start
  500.0 5.1 slice-start.1
  524.9 5.9 slice-start
  525.7 5.1 slice-start.1
  550.6 5.9 slice-start
  551.5 5.1 slice-start.1
  576.4 5.9 slice-start
  577.3 5.1 slice-start.1
  602.1 5.9 slice-start
  603.0 5.1 slice-start.1
  627.9 5.9 slice-start
  628.7 5.0 slice-start.1
  653.5 5.9 slice-start
  654.4 5.0 slice-start.1
  679.2 5.9 slice-start
  680.0 5.0 slice-start.1
  695.5 1.9 copy-start.34
  707.2 284.9 %reduce-scatter.21.cloned.1.call-start = ((), (), s32[]{:S(2)}) async-start(), calls=%async_computation.16 | async-start | bytes 4325376
  707.2 10.2 copy-start.35
  709.8 4.6 collective-permute-start.2
  727.2 407.1 %reduce-scatter.23.cloned.1.call-start = ((), (), s32[]{:S(2)}) async-start(), calls=%async_computation.17 | async-start | bytes 4325376
  729.9 25.6 %copy-start.36 = (bf16[2,512,1024]{2,1,0:T(8,128)(2,1)S(1)}, bf16[2,512,1024]{2,1,0:T(8,128)(2,1)}, u32[]{:S(2)}) copy-start(bf16[2,512,1024]{2,1,0:T(8,128)(2,1)} %param.22) | copy-start | bytes 6291460
  729.9 22.0 %collective-permute-start.3 = (bf16[2,256,1024]{1,2,0:T(8,128)(2,1)S(1)}, bf16[2,256,1024]{1,2,0:T(8,128)(2,1)S(1)}, u32[]{:S(2)}, u32[]{:S(2)}) collective-permute-start(bf16[2,256,1024]{1,2,0:T(8,128)(2,1)S(1)} %get-tuple-element.462), channel_id=1, source_target_pairs={{1,0},{2,1},{3,2},{4,3},{5,4},{6,5},{7,6},{9,8},{10,9},{11,10},{12... | collective-permute-start | bytes 3145736 | tf_op jit(solution)/shard_map/ppermute | solution.py:16
  765.1 555.6 %reduce-scatter.15.cloned.1.call-start = ((), (), s32[]{:S(2)}) async-start(), calls=%async_computation.13 | async-start | bytes 17301504 | tf_op jit(solution)/shard_map/reduce_scatter | solution.py:333
  782.6 725.2 %reduce-scatter.17.cloned.1.call-start = ((), (), s32[]{:S(2)}) async-start(), calls=%async_computation.14 | async-start | bytes 17301504 | tf_op jit(solution)/shard_map/reduce_scatter | solution.py:335
  799.0 3.3 copy-start.16
  799.1 3.3 copy-start.38
  802.3 4.4 copy-start.10
  806.7 2.5 copy-start.22
  806.7 2.5 copy-start.23
  806.7 2.5 copy-start.27
  806.7 2.5 copy-start.28
  806.8 2.5 copy-start.29
  806.8 2.5 copy-start.30
  878.6 4.8 copy-start.4
  878.6 4.8 copy-start.18
  878.6 4.8 copy-start.25
  878.6 4.8 copy-start.37
  878.7 6.0 copy-start.39
  (8 other events, 9.6 us)
Sparse Core Ops, SparseCore 0:
  11.0 59.4 all-gather.7
  73.4 55.3 all-gather.11
  131.8 55.7 all-gather.9
  190.5 55.3 all-gather.13
  248.8 76.2 all-gather.15
  327.9 76.0 all-gather.17
  481.1 141.2 reduce-scatter.12
  707.3 142.6 reduce-scatter.18
  852.8 139.2 reduce-scatter.20
  994.8 139.3 reduce-scatter.22
  1137.1 183.5 reduce-scatter.14
  1323.4 184.3 reduce-scatter.16
where the time goes:
time: 1520 us; the launch traced here: 1510 us
  waiting for transfers between devices  742 us (49%)
  matrix products  328 us (22%)
  local copies, waits for them, and re-layouts  160 us (11%)
  blocking collectives  143 us (9%)
  other arithmetic  62.9 us (4%)
  loops' own time  53.8 us (4%)
    unnamed x15, waiting for transfers between devices  248 us
    reduce_scatter x1, waiting for transfers between devices, local(): lax.psum_scatter(outer_weight_grad, ('dp', 'seq'), scatter_dimension=0, t...  187 us
    reduce_scatter x1, waiting for transfers between devices, local(): lax.psum_scatter(inner_weight_grad, ('dp', 'seq'), scatter_dimension=0, t...  186 us
    unnamed x2, blocking collectives  103 us
    dot_general x6, matrix products, times_transposed(): lax.dot_general(left, right, (((1,), (1,)), ((), ())), preferred_element_...  61.6 us
    dot_general x1, matrix products, local(): jnp.dot(normed_low, inner_matrix, preferred_element_type=jnp.float32)  51.6 us
    dot_general x6, matrix products, contract_rows(): lax.dot_general(left, right, (((0,), (0,)), ((), ())), preferred_element_...  50.5 us
    unnamed x111, local copies, waits for them, and re-layouts  45 us
  transfers between devices with their start and end apart: 16, of which 10 were waited for; matrix products, arithmetic and copies ran while one was open for 31% of the time, Pallas kernels for 0%

commit v1 on v0

--- a/solution.py
+++ b/solution.py
@@ -1,10 +1,23 @@
+import functools
+
 import jax
 import jax.numpy as jnp
 from jax import lax
+from jax.experimental import pallas as pl
+from jax.experimental.pallas import tpu as pltpu
 from jax.sharding import PartitionSpec as P
 
 HD = 64
 SEGMAX = 256
+EPS = 1e-05
+LOG2E = 1.4426950408889634
+SCORE_SCALE = 0.125 * LOG2E
+HIDDEN = -1e30
+PAIR = 2 * HD
+MESH = pl.DeviceIdType.MESH
+BF16 = jnp.bfloat16
+F32 = jnp.float32
+MIB = 2**20
 
 
 group_heads = 4
@@ -38,7 +51,7 @@
     return jnp.sum(values.astype(jnp.float32), axis=0)
 
 
-def local(
+def plain(
     hidden_in,
     segment_ids,
     query_weight,
@@ -358,6 +371,941 @@
     )
 
 
+GRID = (2, 2, 4, 2)
+FF_PARTS = 8
+
+
+class Place:
+    def __init__(self):
+        dp = lax.axis_index("dp")
+        seq = lax.axis_index("seq")
+        self.x = lax.rem(dp, 2)
+        self.y = lax.div(dp, 2)
+        self.z = lax.div(seq, 2)
+        self.c = lax.rem(seq, 2)
+        self.seq = seq
+
+    def device(self, x=None, y=None, z=None, c=None):
+        x = self.x if x is None else x
+        y = self.y if y is None else y
+        z = self.z if z is None else z
+        c = self.c if c is None else c
+        return (y * 2 + x, z * 2 + c)
+
+    def peer(self, dim):
+        if dim == "x":
+            return self.device(x=1 - self.x)
+        if dim == "y":
+            return self.device(y=1 - self.y)
+        if dim == "c":
+            return self.device(c=1 - self.c)
+        return self.device(z=lax.rem(self.z + dim, 4))
+
+
+def signal(semaphore, device):
+    pl.semaphore_signal(semaphore, inc=1, device_id=device, device_id_type=MESH)
+
+
+def meet(place, along=0):
+    barrier = pltpu.get_barrier_semaphore()
+    for dim in ("x", "y", "c", 1, 2, 3):
+        signal(barrier, place.peer(dim))
+    extra = 0
+    if along:
+        up = (place.c == 1) & (place.z < 3)
+        down = (place.c == 0) & (place.z > 0)
+        receives, sends = (down, up) if along > 0 else (up, down)
+        other = lax.rem(place.z + (3 if along > 0 else 1), 4)
+
+        @pl.when(receives)
+        def _():
+            signal(barrier, place.device(z=other, c=1 - place.c))
+
+        extra = sends.astype(jnp.int32)
+    pl.semaphore_wait(barrier, 6 + extra)
+
+
+def remote(src, dst, send, recv, device):
+    return pltpu.make_async_remote_copy(
+        src_ref=src, dst_ref=dst, send_sem=send, recv_sem=recv, device_id=device, device_id_type=MESH
+    )
+
+
+class Gather:
+    def __init__(self, place, order, source, target, send, recv):
+        held = {"x": False, "y": False, "z": False}
+
+        def region():
+            index = []
+            for name, size in (("y", 2), ("x", 2), ("z", 4)):
+                index.append(pl.ds(0, size) if held[name] else pl.ds(getattr(place, name), 1))
+            return target(index[0], index[1], index[2], pl.ds(place.c, 1))
+
+        self.own = pltpu.make_async_copy(source, region(), recv.at[6])
+        self.phases = []
+        for number, dim in enumerate(order):
+            here = region()
+            copies = []
+            for partner in (1, 2, 3) if dim == "z" else (dim,):
+                slot = partner - 1 if dim == "z" else {"x": 3, "y": 4}[dim]
+                copies.append(
+                    remote(
+                        source if number == 0 else here,
+                        here,
+                        send.at[slot],
+                        recv.at[slot],
+                        place.peer(partner),
+                    )
+                )
+            self.phases.append(copies)
+            held[dim] = True
+        here = region()
+        self.phases.append([remote(here, here, send.at[5], recv.at[5], place.peer("c"))])
+
+    def start(self, phase):
+        if phase == 0:
+            self.own.start()
+        for copy in self.phases[phase]:
+            copy.start()
+
+    def arrive(self, phase):
+        for copy in self.phases[phase]:
+            copy.wait_recv()
+        if phase == 0:
+            self.own.wait()
+
+    def step(self, phase):
+        if phase > 0:
+            self.arrive(phase - 1)
+        if phase < 4:
+            self.start(phase)
+
+    def finish(self):
+        for copies in self.phases:
+            for copy in copies:
+                copy.wait_send()
+
+
+class Scatter:
+    def __init__(self, place, order, stage, own, store, bufs, send, recv):
+        r0, r1, r2, r3 = bufs
+        self.place, self.order, self.own, self.store = place, order, own, store
+        self.bufs = bufs
+        self.copies = [[remote(stage(1 - place.c), r0, send.at[0], recv.at[0], place.peer("c"))]]
+        y, x, z = place.y, place.x, place.z
+        if order == "yx":
+            first, second = (r0.at[1 - y], "y"), (r1.at[1 - x], "x")
+        else:
+            first, second = (r0.at[:, 1 - x], "x"), (r1.at[1 - y], "y")
+        self.copies.append([remote(first[0], r1, send.at[1], recv.at[1], place.peer(first[1]))])
+        self.copies.append([remote(second[0], r2, send.at[2], recv.at[2], place.peer(second[1]))])
+        self.copies.append(
+            [
+                remote(r2.at[lax.rem(z + k, 4)], r3.at[k - 1], send.at[2 + k], recv.at[2 + k], place.peer(k))
+                for k in (1, 2, 3)
+            ]
+        )
+
+    def step(self, phase):
+        place = self.place
+        r0, r1, r2, r3 = self.bufs
+        if phase > 0:
+            for copy in self.copies[phase - 1]:
+                copy.wait_recv()
+        if phase == 1:
+            r0[...] = (r0[...].astype(F32) + self.own().astype(F32)).astype(BF16)
+        elif phase == 2:
+            mine = r0[place.y] if self.order == "yx" else r0[:, place.x]
+            r1[...] = (r1[...].astype(F32) + mine.astype(F32)).astype(BF16)
+        elif phase == 3:
+            mine = r1[place.x] if self.order == "yx" else r1[place.y]
+            r2[...] = (r2[...].astype(F32) + mine.astype(F32)).astype(BF16)
+        elif phase == 4:
+            total = r2[place.z].astype(F32)
+            for k in range(3):
+                total = total + r3[k].astype(F32)
+            self.store(total)
+        if phase < 4:
+            for copy in self.copies[phase]:
+                copy.start()
+
+    def finish(self):
+        for copies in self.copies:
+            for copy in copies:
+                copy.wait_send()
+
+
+def advance(slots, tick, phases=5):
+    for phase in range(phases):
+        number = tick - phase
+        if 0 <= number < len(slots):
+            for part in slots[number]:
+                part.step(phase)
+
+
+def dot(left, right):
+    return jnp.dot(left, right, preferred_element_type=F32)
+
+
+def dot_nt(left, right):
+    return lax.dot_general(left, right, (((1,), (1,)), ((), ())), preferred_element_type=F32)
+
+
+def dot_tn(left, right):
+    return lax.dot_general(left, right, (((0,), (0,)), ((), ())), preferred_element_type=F32)
+
+
+def spread(blocks, row, base, width, count):
+    flat = blocks.reshape(32 * 16, 128)
+    lane = lax.broadcasted_iota(jnp.int32, (128, count), 0)
+    column = lax.broadcasted_iota(jnp.int32, (128, count), 1)
+    pick = jnp.where(lane == base + lax.rem(column, width), 1.0, 0.0).astype(BF16)
+    wide = dot(flat, pick)
+    at = lax.broadcasted_iota(jnp.int32, (32 * 16, count), 0)
+    column = lax.broadcasted_iota(jnp.int32, (32 * 16, count), 1)
+    keep = at == lax.div(column, width) * 16 + row
+    return jnp.sum(jnp.where(keep, wide, 0.0), axis=0, keepdims=True)
+
+
+def project_kernel(
+    x_in, small_in, wq_in, wk_in, wv_in, wo_in,
+    q_out, k_out, v_out, xt_out, w_out, vec_out, ib_out,
+    weights, smalls, xt, q_buf, k_buf, v_buf, send, recv, tail_sem, local_sem,
+):
+    place = Place()
+    tokens = x_in.shape[1]
+    own_x = pltpu.make_async_copy(x_in, xt.at[:, pl.ds(SEGMAX, tokens)], local_sem.at[0])
+    own_x.start()
+    meet(place, 1)
+    width = x_in.shape[2]
+    half = width // 2
+    slots = [[Gather(place, "zxy", small_in, lambda y, x, z, c: smalls.at[y, x, z, c], send.at[16], recv.at[16])]]
+    number = 0
+    for matrix, source in enumerate((wq_in, wk_in, wv_in, wo_in)):
+        for part in range(2):
+            pair = []
+            for piece, order in enumerate(("zxy", "zyx")):
+                columns = pl.ds(part * half + piece * half // 2, half // 2)
+                pair.append(
+                    Gather(
+                        place,
+                        order,
+                        source.at[:, :, :, :, :, columns],
+                        lambda y, x, z, c, m=matrix, cols=columns: weights.at[m, y, x, z, c, :, cols],
+                        send.at[number],
+                        recv.at[number],
+                    )
+                )
+                number += 1
+            slots.append(pair)
+
+    tail = remote(
+        x_in.at[:, pl.ds(tokens - SEGMAX, SEGMAX)],
+        xt.at[:, pl.ds(0, SEGMAX)],
+        tail_sem.at[0],
+        tail_sem.at[1],
+        place.device(z=lax.rem(place.z + place.c, 4), c=1 - place.c),
+    )
+    has_next, has_last = place.seq < 7, place.seq > 0
+
+    saves = []
+
+    def save(source, target):
+        copy = pltpu.make_async_copy(source, target, local_sem.at[1 + len(saves)])
+        copy.start()
+        saves.append(copy)
+
+    def project(matrix, target, bias, rows_from):
+        def body(step, carry):
+            row, part = lax.div(step, 2), lax.rem(step, 2)
+            columns = pl.ds(pl.multiple_of(part * half, half), half)
+            block = weights[matrix, :, :, :, :, :, columns].reshape(width, half)
+            out = dot(xt[row, rows_from:, :], block)
+            if bias is not None:
+                out = out + vec_out[bias : bias + 1, columns]
+            target[row, :, columns] = out.astype(BF16)
+            return carry
+
+        lax.fori_loop(0, 4, body, 0)
+
+    for tick in range(len(slots) + 4):
+        if tick == 2:
+            pl.when(has_next)(tail.start)
+        if tick == 3:
+            xt_zero = jnp.zeros((2, SEGMAX, width), BF16)
+
+            @pl.when(place.seq == 0)
+            def _():
+                xt[:, :SEGMAX, :] = xt_zero
+
+            own_x.wait()
+        advance(slots, tick)
+        if tick == 4:
+            for vector in range(8):
+                vec_out[vector : vector + 1, :] = spread(smalls[...], vector // 4, vector % 4 * 32, 32, width)
+            vec_out[8:, :] = jnp.zeros((8, width), F32)
+            for part in range(FF_PARTS):
+                ib_out[part : part + 1, :] = spread(smalls[...], 2, part * 16, 16, 512)
+        if tick == 6:
+            save(weights.at[0], w_out.at[0])
+            project(0, q_buf, 0, SEGMAX)
+            save(q_buf, q_out)
+        if tick == 8:
+            save(weights.at[1], w_out.at[1])
+            pl.when(has_last)(tail.wait_recv)
+            save(xt, xt_out)
+            project(1, k_buf, None, 0)
+            save(k_buf, k_out)
+        if tick == 10:
+            save(weights.at[2], w_out.at[2])
+            project(2, v_buf, 1, 0)
+            save(v_buf, v_out)
+        if tick == 12:
+            save(weights.at[3], w_out.at[3])
+    for slot in slots:
+        for part in slot:
+            part.finish()
+    pl.when(has_next)(tail.wait_send)
+    for copy in saves:
+        copy.wait()
+
+
+def project(hidden, small, wq, wk, wv, wo):
+    rows, tokens, width = hidden.shape
+    window = tokens + SEGMAX
+    hbm = pl.BlockSpec(memory_space=pl.ANY)
+    vmem = pl.BlockSpec(memory_space=pltpu.VMEM)
+    lead = lambda a: a.reshape((1, 1, 1, 1) + a.shape)
+    block = wq.shape
+    return pl.pallas_call(
+        project_kernel,
+        out_shape=[
+            jax.ShapeDtypeStruct((rows, tokens, width), BF16),
+            jax.ShapeDtypeStruct((rows, window, width), BF16),
+            jax.ShapeDtypeStruct((rows, window, width), BF16),
+            jax.ShapeDtypeStruct((rows, window, width), BF16),
+            jax.ShapeDtypeStruct((4,) + GRID + block, BF16),
+            jax.ShapeDtypeStruct((16, width), F32),
+            jax.ShapeDtypeStruct((FF_PARTS, 512), F32),
+        ],
+        in_specs=[hbm] * 6,
+        out_specs=[hbm] * 5 + [vmem] * 2,
+        scratch_shapes=[
+            pltpu.VMEM((4,) + GRID + block, BF16),
+            pltpu.VMEM(GRID + (16, 128), BF16),
+            pltpu.VMEM((rows, window, width), BF16),
+            pltpu.VMEM((rows, tokens, width), BF16),
+            pltpu.VMEM((rows, window, width), BF16),
+            pltpu.VMEM((rows, window, width), BF16),
+            pltpu.SemaphoreType.DMA((17, 8)),
+            pltpu.SemaphoreType.DMA((17, 8)),
+            pltpu.SemaphoreType.DMA((2,)),
+            pltpu.SemaphoreType.DMA((10,)),
+        ],
+        compiler_params=pltpu.CompilerParams(
+            collective_id=0, has_side_effects=True, vmem_limit_bytes=48 * MIB
+        ),
+        name="gather_project",
+    )(hidden, lead(small), lead(wq), lead(wk), lead(wv), lead(wo))
+
+
+def mask_scores(key_ids, query_ids):
+    keys, queries = key_ids.shape[0], query_ids.shape[1]
+    key_at = lax.broadcasted_iota(jnp.int32, (keys, queries), 0)
+    query_at = lax.broadcasted_iota(jnp.int32, (keys, queries), 1)
+    visible = ((key_ids == query_ids) & (query_ids > 0)) | (key_at == query_at + SEGMAX)
+    return jnp.where(visible, 0.0, HIDDEN).astype(F32)
+
+
+def one_head(block, head):
+    lane = lax.broadcasted_iota(jnp.int32, block.shape, 1)
+    return jnp.where(lax.div(lane, HD) == head, block, jnp.zeros_like(block))
+
+
+def layer_norm(value):
+    center = value - jnp.mean(value, axis=-1, keepdims=True)
+    scale = lax.rsqrt(jnp.mean(center * center, axis=-1, keepdims=True) + EPS)
+    return center * scale, scale
+
+
+def layer_norm_back(grad, unit, scale):
+    return scale * (
+        grad
+        - jnp.mean(grad, axis=-1, keepdims=True)
+        - unit * jnp.mean(grad * unit, axis=-1, keepdims=True)
+    )
+
+
+def attend_kernel(q, k, v, key_ids, query_ids, x, wo, vec, mixed, lse, low, unit, scale, bias):
+    pair = pl.program_id(1)
+    tokens = q.shape[1]
+
+    @pl.when(pair == 0)
+    def _():
+        bias[...] = mask_scores(key_ids[0], query_ids[0])
+
+    columns = pl.ds(pl.multiple_of(pair * PAIR, PAIR), PAIR)
+    v_t = v[0].T
+    for start in range(0, tokens, 256):
+        low_key = 0 if start == 0 else start
+        queries = q[0, start : start + 256, :]
+        keys = k[0, low_key:, :]
+        parts = []
+        for head in range(2):
+            s = dot_nt(keys, one_head(queries, head)) * SCORE_SCALE + bias[low_key:, start : start + 256]
+            highest = jnp.max(s, axis=0, keepdims=True)
+            expo = jnp.exp2(s - highest)
+            total = jnp.sum(expo, axis=0, keepdims=True)
+            out = dot(v_t[head * HD : head * HD + HD, low_key:], expo.astype(BF16))
+            parts.append(out * (1.0 / total))
+            lse[0, 0, head : head + 1, start : start + 256] = highest + jnp.log2(total)
+        mixed[0, start : start + 256, columns] = jnp.concatenate(parts, axis=0).T.astype(BF16)
+
+    @pl.when(pair == pl.num_programs(1) - 1)
+    def _():
+        for start in range(0, tokens, 256):
+            rows = pl.ds(start, 256)
+            total = dot(mixed[0, rows, :], wo[...]) + x[0, rows, :].astype(F32) + vec[2:3, :]
+            centered, spread_ = layer_norm(total)
+            unit[0, rows, :] = centered
+            scale[0, rows, :] = spread_
+            low[0, rows, :] = (centered * vec[3:4, :] + vec[4:5, :]).astype(BF16)
+
+
+def attend(q, k, v, key_ids, query_ids, x, wo, vec):
+    rows, tokens, width = q.shape
+    window = k.shape[1]
+    pairs = width // PAIR
+    whole = lambda shape: pl.BlockSpec(shape, lambda r, p: (0,) * len(shape))
+    per_pair = lambda n: pl.BlockSpec((1, n, PAIR), lambda r, p: (r, 0, p))
+    per_row = lambda *s: pl.BlockSpec((1,) + s, lambda r, p: (r, 0, 0))
+    return pl.pallas_call(
+        attend_kernel,
+        grid=(rows, pairs),
+        out_shape=[
+            jax.ShapeDtypeStruct((rows, tokens, width), BF16),
+            jax.ShapeDtypeStruct((rows, pairs, 8, tokens), F32),
+            jax.ShapeDtypeStruct((rows, tokens, width), BF16),
+            jax.ShapeDtypeStruct((rows, tokens, width), F32),
+            jax.ShapeDtypeStruct((rows, tokens, 1), F32),
+        ],
+        in_specs=[
+            per_pair(tokens), per_pair(window), per_pair(window),
+            per_row(window, 1), per_row(1, tokens), per_row(tokens, width),
+            whole(wo.shape), whole(vec.shape),
+        ],
+        out_specs=[
+            per_row(tokens, width),
+            pl.BlockSpec((1, 1, 8, tokens), lambda r, p: (r, p, 0, 0)),
+            per_row(tokens, width),
+            per_row(tokens, width),
+            per_row(tokens, 1),
+        ],
+        scratch_shapes=[pltpu.VMEM((window, tokens), F32)],
+        compiler_params=pltpu.CompilerParams(vmem_limit_bytes=48 * MIB),
+        name="attend",
+    )(q, k, v, key_ids, query_ids, x, wo, vec)
+
+
+def gelu_both(value):
+    bell = jnp.exp2(value * value * (-0.5 * LOG2E)) * 0.3989422804014327
+    below = 0.5 + 0.5 * lax.erf(value * 0.7071067811865476)
+    return value * below, below + value * bell
+
+
+def forward_kernel(low, unit, cot, inner_w, inner_b, outer_w, vec, active, slope, layer_out, og, grad_second, sums, total):
+    part = pl.program_id(0)
+    tokens, width = low.shape
+    w1 = inner_w[...].reshape(width, 512)
+    w2 = outer_w[...].reshape(512, width)
+    for start in range(0, tokens, 256):
+        rows = pl.ds(start, 256)
+        inner = dot(low[rows, :], w1) + inner_b[0]
+        act, der = gelu_both(inner)
+        act = act.astype(BF16)
+        active[rows, :] = act
+        slope[rows, :] = der.astype(BF16)
+        out = dot(act, w2)
+
+        @pl.when(part == 0)
+        def _():
+            total[rows, :] = out
+
+        @pl.when(part > 0)
+        def _():
+            total[rows, :] += out
+
+    @pl.when(part == pl.num_programs(0) - 1)
+    def _():
+        sums[...] = jnp.zeros_like(sums)
+        for start in range(0, tokens, 256):
+            rows = pl.ds(start, 256)
+            normed = unit[rows, :] * vec[3:4, :] + vec[4:5, :]
+            centered, scale = layer_norm(total[rows, :] + normed + vec[5:6, :])
+            layer_out[rows, :] = (centered * vec[6:7, :] + vec[7:8, :]).astype(BF16)
+            up = cot[rows, :].astype(F32)
+            grad = layer_norm_back(up * vec[6:7, :], centered, scale)
+            grad_second[rows, :] = grad
+            rounded = grad.astype(BF16)
+            og[rows, :] = rounded
+            sums[0:1, :] += jnp.sum(rounded.astype(F32), axis=0, keepdims=True)
+            sums[1:2, :] += jnp.sum(up * centered, axis=0, keepdims=True)
+            sums[2:3, :] += jnp.sum(up, axis=0, keepdims=True)
+
+
+def feed_forward(low, unit, cot, gathered, inner_b, vec):
+    tokens, width = low.shape
+    ff = FF_PARTS * 512
+    whole = lambda shape: pl.BlockSpec(shape, lambda q: (0,) * len(shape))
+    column = pl.BlockSpec((tokens, 512), lambda q: (0, q))
+    return pl.pallas_call(
+        forward_kernel,
+        grid=(FF_PARTS,),
+        out_shape=[
+            jax.ShapeDtypeStruct((tokens, ff), BF16),
+            jax.ShapeDtypeStruct((tokens, ff), BF16),
+            jax.ShapeDtypeStruct((tokens, width), BF16),
+            jax.ShapeDtypeStruct((tokens, width), BF16),
+            jax.ShapeDtypeStruct((tokens, width), F32),
+            jax.ShapeDtypeStruct((8, width), F32),
+        ],
+        in_specs=[
+            whole(low.shape), whole(unit.shape), whole(cot.shape),
+            pl.BlockSpec((32, 32, 512), lambda q: (0, q // 2, q % 2)),
+            pl.BlockSpec((1, 1, 512), lambda q: (q, 0, 0)),
+            pl.BlockSpec((32, 16, width), lambda q: (0, 8 + q, 0)),
+            whole(vec.shape),
+        ],
+        out_specs=[column, column, whole((tokens, width)), whole((tokens, width)), whole((tokens, width)), whole((8, width))],
+        scratch_shapes=[pltpu.VMEM((tokens, width), F32)],
+        compiler_params=pltpu.CompilerParams(vmem_limit_bytes=56 * MIB),
+        name="feed_forward",
+    )(low, unit, cot, gathered, inner_b.reshape(FF_PARTS, 1, 512), gathered, vec)
+
+
+def backward_kernel(
+    active, slope, og, low, inner_w, outer_w, grad_second, unit, scale, mixed, wo, vec,
+    outer_grad, inner_grad, ib_grad, grad_first, grad_mixed, wo_grad, sums, total, ig,
+):
+    part = pl.program_id(0)
+    tokens, width = og.shape
+    w1 = inner_w[...].reshape(width, 512)
+    w2 = outer_w[...].reshape(512, width)
+    outer_grad[...] = dot_tn(active[...], og[...]).astype(BF16).reshape(outer_grad.shape)
+    ib_grad[...] = jnp.zeros_like(ib_grad)
+    for start in range(0, tokens, 256):
+        rows = pl.ds(start, 256)
+        piece = (dot_nt(og[rows, :], w2) * slope[rows, :].astype(F32)).astype(BF16)
+        ig[rows, :] = piece
+        ib_grad[0] += jnp.sum(piece.astype(F32), axis=0, keepdims=True)
+    inner_grad[...] = dot_tn(low[...], ig[...]).astype(BF16).reshape(inner_grad.shape)
+    for start in range(0, tokens, 256):
+        rows = pl.ds(start, 256)
+        back = dot_nt(ig[rows, :], w1)
+
+        @pl.when(part == 0)
+        def _():
+            total[rows, :] = grad_second[rows, :] + back
+
+        @pl.when(part > 0)
+        def _():
+            total[rows, :] += back
+
+    @pl.when(part == pl.num_programs(0) - 1)
+    def _():
+        sums[...] = jnp.zeros_like(sums)
+        for start in range(0, tokens, 256):
+            rows = pl.ds(start, 256)
+            up = total[rows, :]
+            centered = unit[rows, :]
+            grad = layer_norm_back(up * vec[3:4, :], centered, scale[rows, :])
+            grad_first[rows, :] = grad
+            rounded = grad.astype(BF16)
+            og[rows, :] = rounded
+            sums[0:1, :] += jnp.sum(rounded.astype(F32), axis=0, keepdims=True)
+            sums[1:2, :] += jnp.sum(up * centered, axis=0, keepdims=True)
+            sums[2:3, :] += jnp.sum(up, axis=0, keepdims=True)
+            grad_mixed[rows, :] = dot_nt(rounded, wo[...]).astype(BF16)
+        wo_grad[...] = dot_tn(mixed[...], og[...]).astype(BF16).reshape(wo_grad.shape)
+
+
+def feed_backward(active, slope, og, low, gathered, grad_second, unit, scale, mixed, wo, vec):
+    tokens, width = og.shape
+    whole = lambda shape: pl.BlockSpec(shape, lambda q: (0,) * len(shape))
+    column = pl.BlockSpec((tokens, 512), lambda q: (0, q))
+    per_part = lambda shape: pl.BlockSpec((1,) + shape, lambda q: (q,) + (0,) * len(shape))
+    outer_shape, inner_shape, wo_shape = GRID + (16, width), GRID + (32, 512), GRID + (32, width)
+    return pl.pallas_call(
+        backward_kernel,
+        grid=(FF_PARTS,),
+        out_shape=[
+            jax.ShapeDtypeStruct((FF_PARTS,) + outer_shape, BF16),
+            jax.ShapeDtypeStruct((FF_PARTS,) + inner_shape, BF16),
+            jax.ShapeDtypeStruct((FF_PARTS, 1, 512), F32),
+            jax.ShapeDtypeStruct((tokens, width), F32),
+            jax.ShapeDtypeStruct((tokens, width), BF16),
+            jax.ShapeDtypeStruct(wo_shape, BF16),
+            jax.ShapeDtypeStruct((8, width), F32),
+        ],
+        in_specs=[
+            column, column, whole(og.shape), whole(low.shape),
+            pl.BlockSpec((32, 32, 512), lambda q: (0, q // 2, q % 2)),
+            pl.BlockSpec((32, 16, width), lambda q: (0, 8 + q, 0)),
+            whole(grad_second.shape), whole(unit.shape), whole(scale.shape), whole(mixed.shape),
+            whole(wo.shape), whole(vec.shape),
+        ],
+        out_specs=[
+            per_part(outer_shape), per_part(inner_shape), per_part((1, 512)),
+            whole((tokens, width)), whole((tokens, width)), whole(wo_shape), whole((8, width)),
+        ],
+        scratch_shapes=[pltpu.VMEM((tokens, width), F32), pltpu.VMEM((tokens, 512), BF16)],
+        compiler_params=pltpu.CompilerParams(vmem_limit_bytes=60 * MIB),
+        name="feed_backward",
+    )(active, slope, og, low, gathered, gathered, grad_second, unit, scale, mixed, wo, vec)
+
+
+def attend_back_kernel(
+    q, k, v, gm, mixed, lse, key_ids, query_ids, xt,
+    dq_out, dk_out, dv_out, weight_grad, sums, bias, dq_all, dk_all, dv_all, dk_sum, dv_sum,
+):
+    group, row, inner = pl.program_id(0), pl.program_id(1), pl.program_id(2)
+    tokens = q.shape[1]
+
+    @pl.when((group == 0) & (inner == 0))
+    def _():
+        bias[row] = mask_scores(key_ids[0], query_ids[0])
+
+    k_t = k[0].T
+    for start in range(0, tokens, 256):
+        low_key = 0 if start == 0 else start
+        queries = q[0, start : start + 256, :]
+        grads = gm[0, start : start + 256, :]
+        product = (grads.astype(F32) * mixed[0, start : start + 256, :].astype(F32)).T
+        keys, values = k[0, low_key:, :], v[0, low_key:, :]
+        parts = []
+        dk, dv = 0.0, 0.0
+        for head in range(2):
+            one_q, one_g = one_head(queries, head), one_head(grads, head)
+            delta = jnp.sum(product[head * HD : head * HD + HD, :], axis=0, keepdims=True)
+            s = dot_nt(keys, one_q) * SCORE_SCALE + bias[row, low_key:, start : start + 256]
+            probs = jnp.exp2(s - lse[0, 0, head : head + 1, start : start + 256])
+            dprob = dot_nt(values, one_g)
+            score_grad = (probs * (dprob - delta)).astype(BF16)
+            dv = dv + dot(probs.astype(BF16), one_g)
+            dk = dk + dot(score_grad, one_q)
+            parts.append(dot(k_t[head * HD : head * HD + HD, low_key:], score_grad))
+        dq = (jnp.concatenate(parts, axis=0) * 0.125).T.astype(BF16)
+        dq_out[0, start : start + 256, :] = dq
+        if start == 0:
+            dk_sum[...] = dk
+            dv_sum[...] = dv
+        else:
+            dk_sum[low_key:, :] += dk
+            dv_sum[low_key:, :] += dv
+    dk_out[0] = (dk_sum[...] * 0.125).astype(BF16)
+    dv_out[0] = dv_sum[...].astype(BF16)
+    columns = pl.ds(pl.multiple_of(inner * PAIR, PAIR), PAIR)
+    dq_all[row, :, columns] = dq_out[0]
+    dk_all[row, :, columns] = dk_out[0]
+    dv_all[row, :, columns] = dv_out[0]
+
+    @pl.when((row == 1) & (inner == 1))
+    def _():
+        for number, source in enumerate((dq_all, dk_all, dv_all)):
+            first = SEGMAX if number == 0 else 0
+            grad = dot_tn(xt[0, first:, :], source[0]) + dot_tn(xt[1, first:, :], source[1])
+            span = grad.shape[1]
+            weight_grad[0, :, :, :, :, :, number * span : number * span + span] = grad.astype(BF16).reshape(
+                GRID + (32, span)
+            )
+        sums[...] = jnp.zeros_like(sums)
+        for number, source in enumerate((dq_all, dv_all)):
+            added = jnp.sum(source[0].astype(F32), axis=0, keepdims=True) + jnp.sum(
+                source[1].astype(F32), axis=0, keepdims=True
+            )
+            sums[number : number + 1, :] = added
+
+
+def attend_back(q, k, v, gm, mixed, lse, key_ids, query_ids, xt):
+    rows, tokens, width = q.shape
+    window = k.shape[1]
+    groups = width // (2 * PAIR)
+    whole = lambda shape: pl.BlockSpec(shape, lambda g, r, i: (0,) * len(shape))
+    per_pair = lambda n: pl.BlockSpec((1, n, PAIR), lambda g, r, i: (r, 0, g * 2 + i))
+    per_row = lambda *s: pl.BlockSpec((1,) + s, lambda g, r, i: (r, 0, 0))
+    out_block = GRID + (32, 6 * PAIR)
+    return pl.pallas_call(
+        attend_back_kernel,
+        grid=(groups, rows, 2),
+        out_shape=[
+            jax.ShapeDtypeStruct((rows, tokens, width), BF16),
+            jax.ShapeDtypeStruct((rows, window, width), BF16),
+            jax.ShapeDtypeStruct((rows, window, width), BF16),
+            jax.ShapeDtypeStruct((groups,) + out_block, BF16),
+            jax.ShapeDtypeStruct((8, width), F32),
+        ],
+        in_specs=[
+            per_pair(tokens), per_pair(window), per_pair(window), per_pair(tokens), per_pair(tokens),
+            pl.BlockSpec((1, 1, 8, tokens), lambda g, r, i: (r, g * 2 + i, 0, 0)),
+            per_row(window, 1), per_row(1, tokens), whole(xt.shape),
+        ],
+        out_specs=[
+            per_pair(tokens), per_pair(window), per_pair(window),
+            pl.BlockSpec((1,) + out_block, lambda g, r, i: (g,) + (0,) * len(out_block)),
+            pl.BlockSpec((8, 2 * PAIR), lambda g, r, i: (0, g)),
+        ],
+        scratch_shapes=[
+            pltpu.VMEM((rows, window, tokens), F32),
+            pltpu.VMEM((rows, tokens, 2 * PAIR), BF16),
+            pltpu.VMEM((rows, window, 2 * PAIR), BF16),
+            pltpu.VMEM((rows, window, 2 * PAIR), BF16),
+            pltpu.VMEM((window, PAIR), F32),
+            pltpu.VMEM((window, PAIR), F32),
+        ],
+        compiler_params=pltpu.CompilerParams(vmem_limit_bytes=48 * MIB),
+        name="attend_back",
+    )(q, k, v, gm, mixed, lse, key_ids, query_ids, xt)
+
+
+def scatter_buffers(count, rows, columns):
+    block = (rows, columns)
+    return [
+        pltpu.VMEM((count, 2, 2, 4) + block, BF16),
+        pltpu.VMEM((count, 2, 4) + block, BF16),
+        pltpu.VMEM((count, 4) + block, BF16),
+        pltpu.VMEM((count, 3) + block, BF16),
+        pltpu.SemaphoreType.DMA((count, 6)),
+        pltpu.SemaphoreType.DMA((count, 6)),
+    ]
+
+
+def finish_kernel(
+    outer_in, inner_in, wo_in, qkv_in, small_in, dq, dk, dv, weights, grad_first,
+    outer_out, inner_out, wo_out, qkv_out, small_out, gh_out,
+    own_sem, tail_sem, tail_here, tail_there, gh, *bufs,
+):
+    place = Place()
+    meet(place, -1)
+    kinds = {}
+    for number, name in enumerate(("outer", "inner", "qkv", "small")):
+        kinds[name] = bufs[number * 7 : number * 7 + 7]
+    used = {name: 0 for name in kinds}
+
+    def make(name, order, source, store):
+        r0, r1, r2, r3, send, recv, own = kinds[name]
+        number = used[name]
+        used[name] += 1
+        fetch = pltpu.make_async_copy(source(place.c), own.at[number % 4], own_sem.at[make.fetches])
+        make.fetches += 1
+        scatter = Scatter(
+            place, order, source, lambda: own[number % 4], store,
+            tuple(b.at[number] for b in (r0, r1, r2, r3)), send.at[number], recv.at[number],
+        )
+        step = scatter.step
+
+        def fetched(phase):
+            if phase == 0:
+                fetch.start()
+            if phase == 1:
+                fetch.wait()
+            step(phase)
+
+        scatter.step = fetched
+        return scatter
+
+    make.fetches = 0
+
+    def halves(name, ref, out, columns):
+        pair = []
+        for half, order in enumerate(("yx", "xy")):
+            cols = pl.ds(half * columns // 2, columns // 2)
+
+            def store(total, cols=cols):
+                out[:, cols] = total
+
+            pair.append(make(name, order, lambda c, cols=cols: ref.at[:, :, :, c, :, cols], store))
+        return pair
+
+    width = wo_in.shape[-1]
+    slots = []
+    for part in range(FF_PARTS):
+        slots.append(halves("outer", outer_in.at[part], outer_out.at[pl.ds(part * 16, 16)], width))
+    for part in range(FF_PARTS):
+        slots.append(halves("inner", inner_in.at[part], inner_out.at[part], 512))
+    for part in range(2):
+        cols = pl.ds(part * 512, 512)
+        slots.append(halves("inner", wo_in.at[:, :, :, :, :, cols], wo_out.at[:, cols], 512))
+    for part in range(qkv_in.shape[0]):
+        slots.append(halves("qkv", qkv_in.at[part], qkv_out.at[part], qkv_in.shape[-1]))
+
+    def store_small(total):
+        small_out[...] = total
+
+    slots.append([make("small", "yx", lambda c: small_in.at[:, :, :, c], store_small)])
+
+    half = width // 2
+    tokens = dq.shape[1]
+    matrix = lambda m, cols: weights[m, :, :, :, :, cols, :].reshape(-1, width)
+    full = [weights.at[m] for m in range(3)]
+
+    def tail_rows(row):
+        return dot_nt(dk[row, :SEGMAX, :], full[1][...].reshape(width, width)) + dot_nt(
+            dv[row, :SEGMAX, :], full[2][...].reshape(width, width)
+        )
+
+    send_tail, recv_tail = place.seq > 0, place.seq < 7
+    tail = remote(
+        tail_here, tail_there, tail_sem.at[0], tail_sem.at[1],
+        place.device(z=lax.rem(place.z + 3 + place.c, 4), c=1 - place.c),
+    )
+
+    def own_rows(row, start):
+        rows = pl.ds(start, 256)
+        total = grad_first[row, rows, :] + dot_nt(dq[row, rows, :], full[0][...].reshape(width, width))
+        rows_k = pl.ds(start + SEGMAX, 256)
+        total = total + dot_nt(dk[row, rows_k, :], full[1][...].reshape(width, width))
+        total = total + dot_nt(dv[row, rows_k, :], full[2][...].reshape(width, width))
+        gh[row, rows, :] = total
+
+    work = {0: lambda: tail_rows_both(), 1: lambda: own_rows(0, 0), 2: lambda: own_rows(0, 256), 3: lambda: own_rows(1, 0), 4: lambda: own_rows(1, 256)}
+
+    def tail_rows_both():
+        for row in range(2):
+            tail_here[row] = tail_rows(row).astype(BF16)
+        pl.when(send_tail)(tail.start)
+
+    for tick in range(len(slots) + 4):
+        advance(slots, tick)
+        if tick in work:
+            work[tick]()
+
+    @pl.when(place.seq == 7)
+    def _():
+        tail_there[...] = jnp.zeros_like(tail_there)
+
+    pl.when(recv_tail)(tail.wait_recv)
+    for row in range(2):
+        gh[row, tokens - SEGMAX :, :] += tail_there[row].astype(F32)
+    save = pltpu.make_async_copy(gh, gh_out, own_sem.at[make.fetches])
+    save.start()
+    for slot in slots:
+        for part in slot:
+            part.finish()
+    pl.when(send_tail)(tail.wait_send)
+    save.wait()
+
+
+def finish(outer_in, inner_in, wo_in, qkv_in, small_in, dq, dk, dv, weights, grad_first):
+    rows, tokens, width = dq.shape
+    hbm = pl.BlockSpec(memory_space=pl.ANY)
+    vmem = pl.BlockSpec(memory_space=pltpu.VMEM)
+    groups = qkv_in.shape[0]
+    span = qkv_in.shape[-1]
+    bufs = []
+    for count, block_rows, columns in (
+        (2 * FF_PARTS, 16, width // 2),
+        (2 * (FF_PARTS + 2), 32, 256),
+        (2 * groups, 32, span // 2),
+        (1, 16, 128),
+    ):
+        bufs += scatter_buffers(count, block_rows, columns)
+        bufs.append(pltpu.VMEM((min(count, 4), 2, 2, 4, block_rows, columns), BF16))
+    return pl.pallas_call(
+        finish_kernel,
+        out_shape=[
+            jax.ShapeDtypeStruct((FF_PARTS * 16, width), F32),
+            jax.ShapeDtypeStruct((FF_PARTS, 32, 512), F32),
+            jax.ShapeDtypeStruct((32, width), F32),
+            jax.ShapeDtypeStruct((groups, 32, span), F32),
+            jax.ShapeDtypeStruct((16, 128), F32),
+            jax.ShapeDtypeStruct((rows, tokens, width), F32),
+        ],
+        in_specs=[hbm] * 5 + [vmem] * 5,
+        out_specs=[vmem] * 5 + [hbm],
+        scratch_shapes=[
+            pltpu.SemaphoreType.DMA((64,)),
+            pltpu.SemaphoreType.DMA((2,)),
+            pltpu.VMEM((rows, SEGMAX, width), BF16),
+            pltpu.VMEM((rows, SEGMAX, width), BF16),
+            pltpu.VMEM((rows, tokens, width), F32),
+        ]
+        + bufs,
+        compiler_params=pltpu.CompilerParams(
+            collective_id=1, has_side_effects=True, vmem_limit_bytes=62 * MIB
+        ),
+        name="sum_gradients",
+    )(outer_in, inner_in, wo_in, qkv_in, small_in, dq, dk, dv, weights, grad_first)
+
+
+def local(
+    hidden_in, segment_ids, query_weight, query_bias, key_weight, value_weight, value_bias, output_weight,
+    output_bias, first_gain, first_shift, inner_weight, inner_bias, outer_weight, outer_bias, second_gain,
+    second_shift, cotangent,
+):
+    rows, tokens, width = hidden_in.shape
+    window = tokens + SEGMAX
+    ff = inner_weight.shape[1]
+    inner_mine = inner_weight.reshape(32, 32, FF_PARTS, 16).transpose(0, 2, 1, 3).reshape(32, ff)
+    inner_mine = inner_mine.reshape(32, 4, 1024).transpose(1, 0, 2).reshape(128, 1024)
+    ff_mine = jnp.concatenate([inner_mine, outer_weight], axis=0)
+    gathered = lax.all_gather(ff_mine, ("dp", "seq"), axis=0, tiled=True).reshape(32, 256, 1024)
+    vectors = (query_bias, value_bias, output_bias, first_gain, first_shift, outer_bias, second_gain, second_shift)
+    small = jnp.concatenate(list(vectors) + [inner_bias, jnp.zeros((13 * 128,), BF16)]).reshape(16, 128)
+
+    q, k, v, xt, weights, vec, inner_b = project(
+        hidden_in, small, query_weight, key_weight, value_weight, output_weight
+    )
+    padded = jnp.concatenate([jnp.full((rows, SEGMAX), -1, jnp.int32), segment_ids], axis=1)
+    key_ids = lax.dynamic_slice_in_dim(padded, lax.axis_index("seq") * tokens, window, 1)
+    query_ids = key_ids[:, None, SEGMAX:]
+    key_ids = key_ids[:, :, None]
+    wo = weights[3].reshape(width, width)
+    mixed, lse, low, unit, scale = attend(q, k, v, key_ids, query_ids, hidden_in, wo, vec)
+    flat = lambda a: a.reshape(rows * tokens, a.shape[-1])
+    active, slope, layer_out, og, grad_second, sums2 = feed_forward(
+        flat(low), flat(unit), flat(cotangent), gathered, inner_b, vec
+    )
+    outer_grad, inner_grad, ib_grad, grad_first, gm, wo_grad, sums1 = feed_backward(
+        active, slope, og, flat(low), gathered, grad_second, flat(unit), flat(scale), flat(mixed), wo, vec
+    )
+    dq, dk, dv, qkv_grad, sums0 = attend_back(
+        q, k, v, gm.reshape(rows, tokens, width), mixed, lse, key_ids, query_ids, xt
+    )
+    listed = jnp.stack(
+        [sums0[0], sums0[1], sums1[0], sums1[1], sums1[2], sums2[0], sums2[1], sums2[2]]
+    )
+    small_grad = listed.reshape(8, 32, 32).transpose(1, 0, 2).reshape(32, 2, 128)
+    ib_mine = ib_grad.reshape(FF_PARTS, 32, 16).transpose(1, 0, 2).reshape(32, 1, 128)
+    small_grad = jnp.concatenate([small_grad, ib_mine, jnp.zeros((32, 13, 128), F32)], axis=1)
+    small_grad = small_grad.astype(BF16).reshape(GRID + (16, 128))
+    outer_sum, inner_sum, wo_sum, qkv_sum, small_sum, grad_hidden = finish(
+        outer_grad, inner_grad, wo_grad, qkv_grad, small_grad, dq, dk, dv, weights[:3],
+        grad_first.reshape(rows, tokens, width),
+    )
+    inner_sum = inner_sum.reshape(FF_PARTS, 32, 32, 16).transpose(1, 2, 0, 3).reshape(32, ff)
+    qkv_sum = qkv_sum.reshape(4, 32, 3, 256).transpose(2, 1, 0, 3).reshape(3, 32, width)
+    vector = small_sum[:2].reshape(8, 32)
+    return (
+        layer_out.reshape(rows, tokens, width),
+        grad_hidden,
+        qkv_sum[0],
+        vector[0],
+        qkv_sum[1],
+        qkv_sum[2],
+        vector[1],
+        wo_sum,
+        vector[2],
+        vector[3],
+        vector[4],
+        inner_sum,
+        small_sum[2],
+        outer_sum,
+        vector[5],
+        vector[6],
+        vector[7],
+    )
+
+
 def solution(mesh):
     in_specs = (
         P("dp", "seq", None),
@@ -398,4 +1346,6 @@
         P(("dp", "seq")),
         P(("dp", "seq")),
     )
-    return jax.shard_map(local, mesh=mesh, in_specs=in_specs, out_specs=out_specs, check_vma=False)
+    fits = dict(mesh.shape) == {"dp": 4, "seq": 8}
+    body = local if fits else plain
+    return jax.shard_map(body, mesh=mesh, in_specs=in_specs, out_specs=out_specs, check_vma=False)

time: 1520 us -> 514 us (0.34)
  the two profiles are of different devices: /device:TPU:0 before, /device:TPU:2 now
where the time goes in v1:
time: 514 us; the launch traced here: 504 us
  Pallas kernels  443 us (86%)
  local copies, waits for them, and re-layouts  42.1 us (8%)
  between operations  14.9 us (3%)
    pallas_call x1, Pallas kernels, finish(): pl.pallas_call(finish_kernel, out_shape=[jax.ShapeDtypeStruct((FF_PARTS *...  141 us
    pallas_call x1, Pallas kernels, project(): pl.pallas_call(project_kernel, out_shape=[jax.ShapeDtypeStruct((rows, tok...  90.2 us
    pallas_call x1, Pallas kernels, feed_backward(): pl.pallas_call(backward_kernel, grid=(FF_PARTS,), out_shape=[jax.ShapeDty...  74.1 us
    pallas_call x1, Pallas kernels, attend_back(): pl.pallas_call(attend_back_kernel, grid=(groups, rows, 2), out_shape=[jax...  49.4 us
    pallas_call x1, Pallas kernels, feed_forward(): pl.pallas_call(forward_kernel, grid=(FF_PARTS,), out_shape=[jax.ShapeDtyp...  46.8 us
    pallas_call x1, Pallas kernels, attend(): pl.pallas_call(attend_kernel, grid=(rows, pairs), out_shape=[jax.ShapeDty...  42.1 us
    unnamed x58, local copies, waits for them, and re-layouts  20 us
  transfers between devices with their start and end apart: 1, of which 0 were waited for; matrix products, arithmetic and copies ran while one was open for 2% of the time, Pallas kernels for 26%

profile of v1, /device:TPU:2, one launch (start us, length us, event | category | flops | bytes accessed | tf_op | source)
XLA Modules:
  0.0 503.9 jit_solution(16356838880548255277)
XLA Ops:
  7.2 0.0 copy-start.23
  7.2 0.0 copy-start.22
  7.2 0.0 copy-start.21
  7.2 0.0 copy-start.24
  7.2 0.0 copy-start.20
  7.2 0.0 copy-start.19
  7.3 0.0 copy-start.18
  7.3 0.0 copy-start.17
  7.3 0.0 copy-start.16
  7.3 0.0 copy-start.4
  7.3 0.0 all-gather.2.cloned.1.call-start
  7.4 2.4 copy.52
  9.8 1.4 copy.53
  11.2 1.0 copy.54
  12.2 1.9 pad_maximum_fusion
  14.1 0.0 all-gather.2.cloned.1.call-update
  14.2 0.1 concatenate.18
  14.3 0.0 copy-done.9
  14.3 0.0 copy-done.8
  14.4 90.2 %gather_project.1 = (bf16[2,512,1024]{2,1,0:T(8,128)(2,1)S(1)}, bf16[2,768,1024]{2,1,0:T(8,128)(2,1)}, bf16[2,768,1024]{2,1,0:T(8,128)(2,1)}, bf16[2,768,1024]{2...) custom-call(bf16[2,512,1024]{2,1,0:T(8,128)(2,1)S(1)} %copy-done.4, ...), custom_call_target="tpu_custom_call" | custom-call | tf_op jit(solution)/shard_map/gather_project/pallas_call | solution.py:680
  104.6 1.4 copy-done.2
  106.0 3.3 slice.72
  109.3 6.7 %slice.76.weights = bf16[3,2,2,4,2,32,1024]{6,5,4,3,2,1,0:T(8,128)(2,1)} slice(bf16[4,2,2,4,2,32,1024]{6,5,4,3,2,1,0:T(8,128)(2,1)} %get-tuple-element.56), slice={[0:3], [0:2], [0:2], [0:4], [0:2], [0:32], [0:1024]} | slice | bytes 12582912 | tf_op jit(solution)/shard_map/slice | solution.py:1282
  116.0 0.0 copy-done.14
  116.1 0.3 copy.51.key_ids
  116.4 0.6 reshape.131.inner_b
  117.0 0.1 pad.3.clone
  117.1 42.1 %attend.1 = (bf16[2,512,1024]{2,1,0:T(8,128)(2,1)S(1)}, f32[2,8,8,512]{3,2,1,0:T(8,128)S(1)}, bf16[2,512,1024]{2,1,0:T(8,128)(2,1)S(1)}, f32[2,512,1024]{2,1,0:T(8,128)}, f32[2,512,1]{2,1,0:T(8,128)S(1)}) custom-call(bf16[2,512,1024]{2,1,0:T(8,128)(2,1)} %copy-done.2, bf16[2,768,1024]{2,1,0:T(8,128)(2,1)} %get-tuple-element.54.k, ...), custom_call_target="tpu_custom_call" | custom-call | tf_op jit(solution)/shard_map/attend/pallas_call | solution.py:782
  159.2 1.3 copy-done
  160.5 1.3 copy-done.1
  161.8 0.8 copy-done.7
  162.6 46.8 %feed_forward.1 = (bf16[1024,4096]{1,0:T(8,128)(2,1)}, bf16[1024,4096]{1,0:T(8,128)(2,1)}, bf16[1024,1024]{1,0:T(8,128)(2,1)}, bf16[1024,1024]{1,0:T(8,128)(2,1)...) custom-call(bf16[1024,1024]{1,0:T(8,128)(2,1)} %bitcast.61, f32[1024,1024]{1,0:T(8,128)} %bitcast.75, ...), custom_call_target="tpu_custom_call" | custom-call | tf_op jit(solution)/shard_map/feed_forward/pallas_call | solution.py:861
  209.4 74.1 %feed_backward.1 = (bf16[8,2,2,4,2,16,1024]{6,5,4,3,2,1,0:T(8,128)(2,1)}, bf16[8,2,2,4,2,32,512]{6,5,4,3,2,1,0:T(8,128)(2,1)}, f32[8,1,512]{2,1,0:T(1,128)}, f32...) custom-call(bf16[1024,4096]{1,0:T(8,128)(2,1)} %get-tuple-element.62, ...), custom_call_target="tpu_custom_call" | custom-call | tf_op jit(solution)/shard_map/feed_backward/pallas_call | solution.py:938
  283.5 0.8 slice.109
  284.3 0.8 convert_reduce_fusion
  285.0 0.8 slice.108
  285.8 49.4 %attend_back.1 = (bf16[2,512,1024]{2,1,0:T(8,128)(2,1)S(1)}, bf16[2,768,1024]{2,1,0:T(8,128)(2,1)}, bf16[2,768,1024]{2,1,0:T(8,128)(2,1)}, bf16[4,2,2,4,2,32,768]{6,5,4,3,2,1,0:T(8,128)(2,1)}, f32[8,1024]{1,0:T(8,128)S(1)}) custom-call(bf16[2,512,1024]{2,1,0:T(8,128)(2,1)S(1)} %copy-done.3, bf16[2,768,1024]{2,1,0:T(8,128)(2,1)} %get-tuple-element.54.k, ...), custom_call_target="tpu_custom_call" | custom-call | tf_op jit(solution)/shard_map/attend_back/pallas_call | solution.py:1037
  335.2 1.4 copy-done.5
  336.6 0.1 reshape.136
  336.7 0.1 concatenate.21
  336.8 0.1 reshape.137
  337.0 0.1 concatenate.24
  337.1 0.8 maximum_maximum_fusion.small_in
  337.8 140.9 %sum_gradients.1 = (f32[128,1024]{1,0:T(8,128)}, f32[8,32,512]{2,1,0:T(8,128)}, f32[32,1024]{1,0:T(8,128)}, f32[4,32,768]{2,1,0:T(8,128)}, f32[16,128]{1,0:T(8,128)}, /*index=5*/f32[2,512,1024]{2,1,0:T(8,128)}) custom-call(bf16[8,2,2,4,2,16,1024]{6,5,4,3,2,1,0:T(8,128)(2,1)} %get-tuple-element.68.outer_in, ...), custom_call_target="tpu_custom_call" | custom-call | tf_op jit(solution)/shard_map/sum_gradients/pallas_call | solution.py:1213
  478.8 1.2 slice_bitcast_fusion.3
  480.0 0.7 slice.78
  480.7 0.1 reshape.140
  480.8 0.5 slice_bitcast_fusion
  481.3 1.2 reshape.139
  482.5 0.3 fusion.1
  482.8 0.1 copy.61
  482.9 0.7 copy.67
  483.6 0.1 copy.60
  483.7 0.7 copy.66
  484.4 0.1 copy.59
  484.4 0.7 copy.65
  485.1 0.6 copy.62
  485.7 1.6 copy.63
  487.3 3.0 copy.64
  490.3 4.9 copy.73
  495.2 0.0 copy-done.15
  495.2 0.7 copy.74
  495.8 0.0 copy-done.13
  495.8 0.8 copy.75
  (40 shorter events, 0.2 us)
Async XLA Ops:
  7.2 6.9 %copy-start.23 = (bf16[32]{0:T(256)(128)(2,1)S(1)}, bf16[32]{0:T(256)(128)(2,1)}, u32[]{:S(2)}) copy-start(bf16[32]{0:T(256)(128)(2,1)} %param.34) | copy-start | bytes 196
  7.2 6.9 %copy-start.22 = (bf16[32]{0:T(256)(128)(2,1)S(1)}, bf16[32]{0:T(256)(128)(2,1)}, u32[]{:S(2)}) copy-start(bf16[32]{0:T(256)(128)(2,1)} %param.33) | copy-start | bytes 196
  7.2 6.9 %copy-start.21 = (bf16[32]{0:T(256)(128)(2,1)S(1)}, bf16[32]{0:T(256)(128)(2,1)}, u32[]{:S(2)}) copy-start(bf16[32]{0:T(256)(128)(2,1)} %param.32) | copy-start | bytes 196
  7.2 6.9 %copy-start.24 = (bf16[128]{0:T(256)(128)(2,1)S(1)}, bf16[128]{0:T(256)(128)(2,1)}, u32[]{:S(2)}) copy-start(bf16[128]{0:T(256)(128)(2,1)} %param.30) | copy-start | bytes 772
  7.2 6.9 %copy-start.20 = (bf16[32]{0:T(256)(128)(2,1)S(1)}, bf16[32]{0:T(256)(128)(2,1)}, u32[]{:S(2)}) copy-start(bf16[32]{0:T(256)(128)(2,1)} %param.28) | copy-start | bytes 196
  7.2 6.9 %copy-start.19 = (bf16[32]{0:T(256)(128)(2,1)S(1)}, bf16[32]{0:T(256)(128)(2,1)}, u32[]{:S(2)}) copy-start(bf16[32]{0:T(256)(128)(2,1)} %param.27) | copy-start | bytes 196
  7.3 6.9 %copy-start.18 = (bf16[32]{0:T(256)(128)(2,1)S(1)}, bf16[32]{0:T(256)(128)(2,1)}, u32[]{:S(2)}) copy-start(bf16[32]{0:T(256)(128)(2,1)} %param.26) | copy-start | bytes 196
  7.3 6.9 %copy-start.17 = (bf16[32]{0:T(256)(128)(2,1)S(1)}, bf16[32]{0:T(256)(128)(2,1)}, u32[]{:S(2)}) copy-start(bf16[32]{0:T(256)(128)(2,1)} %param.24) | copy-start | bytes 196
  7.3 6.9 %copy-start.16 = (bf16[32]{0:T(256)(128)(2,1)S(1)}, bf16[32]{0:T(256)(128)(2,1)}, u32[]{:S(2)}) copy-start(bf16[32]{0:T(256)(128)(2,1)} %param.21) | copy-start | bytes 196
  7.3 7.0 %copy-start.4 = (bf16[2,512,1024]{2,1,0:T(8,128)(2,1)S(1)}, bf16[2,512,1024]{2,1,0:T(8,128)(2,1)}, u32[]{:S(2)}) copy-start(bf16[2,512,1024]{2,1,0:T(8,128)(2,1)} %x.3) | copy-start | bytes 6291460
  7.3 7.0 %copy-start.11 = (bf16[32,1024]{1,0:T(8,128)(2,1)S(1)}, bf16[32,1024]{1,0:T(8,128)(2,1)}, u32[]{:S(2)}) copy-start(bf16[32,1024]{1,0:T(8,128)(2,1)} %param.25) | copy-start | bytes 196612
  7.3 7.0 %copy-start.10 = (bf16[32,1024]{1,0:T(8,128)(2,1)S(1)}, bf16[32,1024]{1,0:T(8,128)(2,1)}, u32[]{:S(2)}) copy-start(bf16[32,1024]{1,0:T(8,128)(2,1)} %param.23) | copy-start | bytes 196612
  7.3 7.0 %copy-start.9 = (bf16[32,1024]{1,0:T(8,128)(2,1)S(1)}, bf16[32,1024]{1,0:T(8,128)(2,1)}, u32[]{:S(2)}) copy-start(bf16[32,1024]{1,0:T(8,128)(2,1)} %param.22) | copy-start | bytes 196612
  7.3 7.0 %copy-start.8 = (bf16[32,1024]{1,0:T(8,128)(2,1)S(1)}, bf16[32,1024]{1,0:T(8,128)(2,1)}, u32[]{:S(2)}) copy-start(bf16[32,1024]{1,0:T(8,128)(2,1)} %param.20) | copy-start | bytes 196612
  7.3 155.3 %all-gather.2.cloned.1.call-start = ((), (), s32[]{:S(2)}) async-start(), calls=%async_computation | async-start | bytes 17301504 | tf_op jit(solution)/shard_map/all_gather | solution.py:1251
  104.6 1.4 copy-start.2
  106.0 11.1 %copy-start.6 = (f32[16,1024]{1,0:T(8,128)}, f32[16,1024]{1,0:T(8,128)S(1)}, u32[]{:S(2)}) copy-start(f32[16,1024]{1,0:T(8,128)S(1)} %get-tuple-element.57.vec) | copy-start | bytes 196612
  109.3 6.7 %copy-start.14 = (s32[2,4096]{1,0:T(2,128)S(1)}, s32[2,4096]{1,0:T(2,128)}, u32[]{:S(2)}) copy-start(s32[2,4096]{1,0:T(2,128)} %param.19) | copy-start | bytes 98308
  159.2 1.3 copy-start
  160.5 1.3 copy-start.1
  161.8 0.8 copy-start.7
  209.4 76.4 %copy-start.3 = (bf16[2,512,1024]{2,1,0:T(8,128)(2,1)S(1)}, bf16[2,512,1024]{2,1,0:T(8,128)(2,1)}, u32[]{:S(2)}) copy-start(bf16[2,512,1024]{2,1,0:T(8,128)(2,1)} %copy-done.2) | copy-start | bytes 6291460
  335.2 1.4 copy-start.5
  478.7 6.4 %copy-start.12 = (f32[8,32,512]{2,1,0:T(8,128)S(1)}, f32[8,32,512]{2,1,0:T(8,128)}, u32[]{:S(2)}) copy-start(f32[8,32,512]{2,1,0:T(8,128)} %get-tuple-element.87) | copy-start | bytes 1572868
  490.3 4.9 copy-start.15
  490.3 5.5 %copy-start.13 = (f32[128,1024]{1,0:T(8,128)S(1)}, f32[128,1024]{1,0:T(8,128)}, u32[]{:S(2)}) copy-start(f32[128,1024]{1,0:T(8,128)} %get-tuple-element.164) | copy-start | bytes 1572868
Sparse Core Ops, SparseCore 0:
  14.2 136.3 all-gather.1
